TPU v7x, 128 devices: a whole 4x4x4 slice. The times are simulated.
128 devices in a mesh: seq: 8 (over z, core), head: 16 (over y, x).
Axes of the slice: x: 4, y: 4, z: 4, core: 2. Of those that a mesh axis runs over, the one named last changes fastest.
Arguments:
- queries: bfloat16 [16384, 2048], P(('seq', 'head')), may hold values from -6 to 6
- key_rows: bfloat16 [16384, 2048], P(('seq', 'head')), may hold values from -6 to 6
- value_rows: bfloat16 [16384, 2048], P(('seq', 'head')), may hold values from -6 to 6
- ridge_diag: float32 [16, 128], replicated, may hold values from 0.5 to 4
Outputs:
- mixed: bfloat16 [16384, 2048], P(('seq', 'head'))
All inputs are finite; a program needn't handle non-finite values.
Results may differ from a plain program's by a relative error of at most 0.0075.
The roundings to bfloat16 on the way count: a program that leaves them out, or rounds other values in their place, can miss the bound.
Values may be sent and summed in bfloat16 or wider, within the bound.
No kernel may reach another device: no remote copies, remote signals or barrier semaphores. Data moves between devices by JAX's collectives and lax.ppermute only.
A program may use at most 64 MiB of HBM per device.

v0:
```python
import jax
import jax.numpy as jnp
from jax import lax
from jax.sharding import PartitionSpec as P

HEADS = 16
DK = 128
GROUP = 64


epsilon = 1e-06
highest = lax.Precision.HIGHEST


def prefix_2(value, axis, join, neutral):
    count, mine = (lax.axis_size(axis), lax.axis_index(axis))
    pieces = jax.tree.map(lambda part: lax.all_gather(part, axis), value)
    running = jax.tree.map(
        lambda part, zero: jnp.full_like(part, 0) + jnp.asarray(zero, part.dtype), value, neutral
    )

    def turn(position, running):
        longer = join(running, jax.tree.map(lambda part: part[position], pieces))
        return jax.tree.map(lambda new, old: jnp.where(position < mine, new, old), longer, running)

    return lax.fori_loop(0, count - 1, turn, running)


def unit_rows(matrix):
    values_f = matrix.astype(jnp.float32)
    scale_back = lax.rsqrt(jnp.sum(values_f * values_f, axis=-1, keepdims=True) + epsilon)
    return (values_f * scale_back).astype(jnp.bfloat16)


def add_pair(earlier, later):
    return (earlier[0] + later[0], earlier[1] + later[1])


def times_plain(left, right):
    return jnp.einsum("...ij,...jk->...ik", left, right, precision=highest)


def times_turned(left, right):
    return jnp.einsum("...ij,...kj->...ik", left, right, precision=highest)


def turned_times(left, right):
    return jnp.einsum("...ji,...jk->...ik", left, right, precision=highest)


def factor_solve(system, targets):
    width = system.shape[-1]
    edge = min(32, width)
    count = width // edge

    def part(i, j):
        return system[..., i * edge : (i + 1) * edge, j * edge : (j + 1) * edge]

    lower = {}
    inverses = []
    for j in range(count):
        pivot = part(j, j)
        for k in range(j):
            pivot = pivot - times_turned(lower[j, k], lower[j, k])
        pivot_factor = jnp.linalg.cholesky(pivot)
        identity = jnp.broadcast_to(jnp.eye(edge, dtype=jnp.float32), pivot_factor.shape)
        inverse = jax.scipy.linalg.solve_triangular(pivot_factor, identity, lower=True)
        inverses.append(inverse)
        for i in range(j + 1, count):
            below = part(i, j)
            for k in range(j):
                below = below - times_turned(lower[i, k], lower[j, k])
            lower[i, j] = times_turned(below, inverse)
    forward = []
    for j in range(count):
        rest = targets[..., j * edge : (j + 1) * edge, :]
        for k in range(j):
            rest = rest - times_plain(lower[j, k], forward[k])
        forward.append(times_plain(inverses[j], rest))
    backward = [None] * count
    for j in reversed(range(count)):
        rest = forward[j]
        for k in range(j + 1, count):
            rest = rest - turned_times(lower[k, j], backward[k])
        backward[j] = turned_times(inverses[j], rest)
    return jnp.concatenate(backward, axis=-2)


def mesa_block(queries, key_rows, value_rows, ridge_here, prefix):
    row_count = queries.shape[0]
    heads_here = queries.shape[1] // DK
    groups = row_count // GROUP

    def by_group(matrix):
        return jnp.transpose(matrix.reshape(groups, GROUP, heads_here, DK), (2, 0, 1, 3))

    q_unit = by_group(unit_rows(queries.reshape(row_count, heads_here, DK)))
    k_unit = by_group(unit_rows(key_rows.reshape(row_count, heads_here, DK)))
    v_block = by_group(value_rows)
    group_gram = jnp.einsum("hcti,hctj->hcij", k_unit, k_unit, preferred_element_type=jnp.float32)
    group_vk = jnp.einsum("hctv,hctk->hcvk", v_block, k_unit, preferred_element_type=jnp.float32)
    gram_inc = jnp.cumsum(group_gram, axis=1)
    vk_inc = jnp.cumsum(group_vk, axis=1)
    gram_pre, vk_pre = prefix((gram_inc[:, -1], vk_inc[:, -1]))
    gram_start = gram_pre[:, None] + gram_inc - group_gram
    vk_start = vk_pre[:, None] + vk_inc - group_vk
    system = gram_start + ridge_here[:, None, :, None] * jnp.eye(DK, dtype=jnp.float32)
    targets = jnp.swapaxes(q_unit.astype(jnp.float32), -1, -2)
    solved = factor_solve(system, targets)
    k_f = k_unit.astype(jnp.float32)
    carried = jnp.einsum("hcvk,hckt->hctv", vk_start, solved, precision=highest)
    scores = jnp.einsum("hcsk,hckt->hcts", k_f, solved, precision=highest)
    causal = jnp.arange(GROUP)[None, :] <= jnp.arange(GROUP)[:, None]
    within = jnp.einsum(
        "hcts,hcsv->hctv",
        jnp.where(causal, scores, 0.0),
        v_block.astype(jnp.float32),
        precision=highest,
    )
    result = (carried + within).astype(jnp.bfloat16)
    return jnp.transpose(result, (1, 2, 0, 3)).reshape(row_count, heads_here * DK)


def body(queries, key_rows, value_rows, ridge_diag):
    q_heads, k_heads, v_heads = (
        lax.all_to_all(queries, "head", split_axis=1, concat_axis=0, tiled=True),
        lax.all_to_all(key_rows, "head", split_axis=1, concat_axis=0, tiled=True),
        lax.all_to_all(value_rows, "head", split_axis=1, concat_axis=0, tiled=True),
    )
    per_device = HEADS // lax.axis_size("head")
    ridge_here = lax.dynamic_slice_in_dim(
        ridge_diag, lax.axis_index("head") * per_device, per_device, 0
    )

    def head_scan(totals):
        empty = (jnp.zeros_like(totals[0]), jnp.zeros_like(totals[1]))
        return prefix_2(totals, "seq", add_pair, empty)

    result = mesa_block(q_heads, k_heads, v_heads, ridge_here, head_scan)
    return lax.all_to_all(result, "head", split_axis=0, concat_axis=1, tiled=True)


def solution(mesh):
    in_specs = (P(("seq", "head"), None), P(("seq", "head"), None), P(("seq", "head"), None), P())
    out_specs = P(("seq", "head"), None)
    return jax.shard_map(body, mesh=mesh, in_specs=in_specs, out_specs=out_specs, check_vma=False)
```

profile of v0, /device:TPU:0, one launch (start us, length us, event | category | flops | bytes accessed | tf_op | source)
XLA Modules:
  0.0 648.4 jit_solution(9460381625180959422)
XLA Ops:
  0.0 1.4 copy.338
  2.4 7.1 %all-to-all-start = ((bf16[128,16,128]{2,0,1:T(8,128)(2,1)}), bf16[128,16,128]{2,0,1:T(8,128)(2,1)S(1)}, u32[]{:S(2)}, u32[]{:S(2)}) async-start(bf16[128,16,128]{2,0,1:T(8,128)(2,1)} %copy.339), calls=%async_computation | async-start | bytes 1048576 | tf_op jit(solution)/shard_map/all_to_all | solution.py:127
  12.3 8.8 %all-to-all-done = bf16[128,16,128]{2,0,1:T(8,128)(2,1)S(1)} async-done(((bf16[128,16,128]{2,0,1:T(8,128)(2,1)}), bf16[128,16,128]{2,0,1:T(8,128)(2,1)S(1)}, u32[]{:S(2)}, u32[]{:S(2)}) %all-to-all-start) | async-done | bytes 524320 | tf_op jit(solution)/shard_map/all_to_all | solution.py:127
  21.1 4.3 all-to-all-start.1
  26.7 1.9 copy.346
  28.6 1.5 fusion.7
  30.1 3.0 copy.345
  33.0 15.4 %all_gather.6 = f32[8,1,128,128]{3,2,1,0:T(8,128)} all-gather(f32[1,1,128,128]{3,2,1,0:T(8,128)S(1)} %slice-done), channel_id=1, replica_groups=mesh['seq'=8,'head'=16] {'seq'}, dimensions={0}, use_global_device_ids=true | all-gather | bytes 589824 | tf_op jit(solution)/shard_map/all_gather | solution.py:17
  48.4 7.1 %all-to-all-start.2 = ((bf16[128,16,128]{0,2,1:T(8,128)(2,1)}), bf16[128,16,128]{0,2,1:T(8,128)(2,1)}, u32[]{:S(2)}, u32[]{:S(2)}) async-start(bf16[128,16,128]{0,2,1:T(8,128)(2,1)} %bitcast.17), calls=%async_computation.2 | async-start | bytes 1048576 | tf_op jit(solution)/shard_map/all_to_all | solution.py:126
  55.6 1.5 fusion.64
  57.1 2.0 copy.343
  59.1 3.1 fusion.62
  63.0 13.3 %all_gather.7 = f32[8,1,128,128]{3,2,1,0:T(8,128)S(1)} all-gather(f32[1,1,128,128]{3,2,1,0:T(8,128)S(1)} %slice.73), channel_id=1, replica_groups=mesh['seq'=8,'head'=16] {'seq'}, dimensions={0}, use_global_device_ids=true | all-gather | bytes 589824 | tf_op jit(solution)/shard_map/all_gather | solution.py:17
  76.3 6.4 while.16
  82.7 2.6 fusion.5
  85.7 94.4 %custom-call.14 = f32[1,32,32,32]{3,2,1,0:T(8,128)} custom-call(f32[1,32,32,32]{3,2,1,0:T(8,128)S(1)} %fusion.46), custom_call_target="Cholesky" | custom-call | tf_op jit(solution)/shard_map/jit(cholesky)/cholesky | solution.py:65
  180.1 1.3 copy.348
  182.7 13.4 %custom-call.15 = f32[32,1,32,32]{0,2,3,1:T(8,128)S(1)} custom-call(f32[32,1,32,32]{0,3,2,1:T(8,128)} %select_bitcast_fusion.3), custom_call_target="InvertDiagBlocksLowerTriangular" | custom-call | tf_op jit(solution)/shard_map/jit(_solve_triangular)/vmap()/triangular_solve | solution.py:67
  197.3 1.3 fusion.40
  198.5 1.3 fusion.42
  199.8 1.3 fusion.41
  201.1 1.8 fusion.15
  202.8 1.8 fusion.29
  204.6 2.0 copy.356
  206.6 2.1 fusion.45
  208.7 95.1 %custom-call.16 = f32[1,32,32,32]{3,2,1,0:T(8,128)} custom-call(f32[1,32,32,32]{3,2,1,0:T(8,128)} %fusion.45), custom_call_target="Cholesky" | custom-call | tf_op jit(solution)/shard_map/jit(cholesky)/cholesky | solution.py:65
  303.8 2.1 copy.357
  306.0 1.2 select_reduce_fusion.2
  307.2 2.0 select_bitcast_fusion.2
  309.3 14.4 %custom-call.17 = f32[32,1,32,32]{0,2,3,1:T(8,128)} custom-call(f32[32,1,32,32]{0,3,2,1:T(8,128)} %select_bitcast_fusion.2), custom_call_target="InvertDiagBlocksLowerTriangular" | custom-call | tf_op jit(solution)/shard_map/jit(_solve_triangular)/vmap()/triangular_solve | solution.py:67
  323.7 2.3 copy.359
  326.0 1.7 fusion.52
  327.7 2.2 fusion.19
  332.0 1.7 convolution_bitcast_fusion.12
  333.7 1.8 convolution_bitcast_fusion.7
  335.5 1.8 convolution_bitcast_fusion.5
  337.3 2.1 convert_bitcast_fusion
  339.4 2.6 copy.352
  342.0 3.2 copy.353
  346.4 2.1 fusion.60
  350.6 1.5 convolution_bitcast_fusion.10
  352.0 1.5 convolution_bitcast_fusion.2
  353.5 3.3 copy.393
  356.8 2.9 fusion.27
  359.7 1.7 fusion.21
  361.4 2.0 copy.365
  363.5 2.1 fusion.44
  365.6 95.1 %custom-call.18 = f32[1,32,32,32]{3,2,1,0:T(8,128)} custom-call(f32[1,32,32,32]{3,2,1,0:T(8,128)} %fusion.44), custom_call_target="Cholesky" | custom-call | tf_op jit(solution)/shard_map/jit(cholesky)/cholesky | solution.py:65
  460.6 2.1 copy.366
  462.8 1.2 select_reduce_fusion.1
  464.1 2.0 select_bitcast_fusion.1
  466.1 14.2 %custom-call.19 = f32[32,1,32,32]{0,2,3,1:T(8,128)} custom-call(f32[32,1,32,32]{0,3,2,1:T(8,128)} %select_bitcast_fusion.1), custom_call_target="InvertDiagBlocksLowerTriangular" | custom-call | tf_op jit(solution)/shard_map/jit(_solve_triangular)/vmap()/triangular_solve | solution.py:67
  480.3 2.3 copy.368
  482.6 1.7 fusion.50
  485.1 2.1 fusion.69
  488.9 1.8 fusion.32
  493.1 93.8 %custom-call.20 = f32[1,32,32,32]{3,2,1,0:T(8,128)S(1)} custom-call(f32[1,32,32,32]{3,2,1,0:T(8,128)S(1)} %fusion.43), custom_call_target="Cholesky" | custom-call | tf_op jit(solution)/shard_map/jit(cholesky)/cholesky | solution.py:65
  587.6 12.6 %custom-call.21 = f32[32,1,32,32]{0,2,3,1:T(8,128)S(1)} custom-call(f32[32,1,32,32]{0,3,2,1:T(8,128)S(1)} %select_bitcast_fusion), custom_call_target="InvertDiagBlocksLowerTriangular" | custom-call | tf_op jit(solution)/shard_map/jit(_solve_triangular)/vmap()/triangular_solve | solution.py:67
  601.4 1.7 fusion.24
  604.5 1.7 fusion.36
  617.4 1.9 convolution_select_fusion
  619.4 2.8 fusion.74
  622.3 6.1 fusion.12
  628.3 19.0 %all_to_all.61 = bf16[16,128,128]{2,1,0:T(8,128)(2,1)S(1)} all-to-all(bf16[16,128,128]{2,1,0:T(8,128)(2,1)S(1)} %bitcast.306), channel_id=1, replica_groups=mesh['seq'=8,'head'=16] {'head'}, dimensions={0} | all-to-all | bytes 1048576 | tf_op jit(solution)/shard_map/all_to_all | solution.py:140
  (150 shorter events, 40.3 us)
Async XLA Ops:
  0.0 11.3 %copy-start = (bf16[128,2048]{1,0:T(8,128)(2,1)S(1)}, bf16[128,2048]{1,0:T(8,128)(2,1)}, u32[]{:S(2)}) copy-start(bf16[128,2048]{1,0:T(8,128)(2,1)} %param.11) | copy-start | bytes 1572868
  0.0 10.3 %copy-start.38 = (bf16[128,2048]{1,0:T(8,128)(2,1)S(1)}, bf16[128,2048]{1,0:T(8,128)(2,1)}, u32[]{:S(2)}) copy-start(bf16[128,2048]{1,0:T(8,128)(2,1)} %param.9) | copy-start | bytes 1572868
  2.4 18.7 %all-to-all-start = ((bf16[128,16,128]{2,0,1:T(8,128)(2,1)}), bf16[128,16,128]{2,0,1:T(8,128)(2,1)S(1)}, u32[]{:S(2)}, u32[]{:S(2)}) async-start(bf16[128,16,128]{2,0,1:T(8,128)(2,1)} %copy.339), calls=%async_computation | async-start | bytes 1048576 | tf_op jit(solution)/shard_map/all_to_all | solution.py:127
  21.1 27.3 %all-to-all-start.1 = ((bf16[128,16,128]{2,0,1:T(8,128)(2,1)}), bf16[128,16,128]{2,0,1:T(8,128)(2,1)}, u32[]{:S(2)}, u32[]{:S(2)}) async-start(bf16[128,16,128]{2,0,1:T(8,128)(2,1)} %copy_bitcast_fusion.1), calls=%async_computation.1 | async-start | bytes 1048576 | tf_op jit(solution)/shard_map/all_to_all | solution.py:128
  26.2 29.3 %copy-start.25 = (bf16[32,64,128]{2,1,0:T(8,128)(2,1)}, bf16[32,64,128]{2,1,0:T(8,128)(2,1)S(1)}, u32[]{:S(2)}) copy-start(bf16[32,64,128]{2,1,0:T(8,128)(2,1)S(1)} %multiply_convert_fusion.1) | copy-start | bytes 1572868
  30.1 3.0 slice-start
  48.4 288.9 %all-to-all-start.2 = ((bf16[128,16,128]{0,2,1:T(8,128)(2,1)}), bf16[128,16,128]{0,2,1:T(8,128)(2,1)}, u32[]{:S(2)}, u32[]{:S(2)}) async-start(bf16[128,16,128]{0,2,1:T(8,128)(2,1)} %bitcast.17), calls=%async_computation.2 | async-start | bytes 1048576 | tf_op jit(solution)/shard_map/all_to_all | solution.py:126
  57.1 2.0 copy-start.14
  197.3 2.5 copy-start.5
  199.8 3.0 copy-start.2
  326.0 3.9 copy-start.36
  327.7 4.3 copy-start.16
  330.9 4.6 copy-start.8
  332.0 1.8 copy-start.11
  346.4 2.1 copy-start.6
  346.4 2.5 copy-start.3
  348.4 2.1 copy-start.30
  348.5 1.4 copy-start.17
  348.9 3.2 copy-start.21
  348.9 1.7 copy-start.12
  349.9 2.2 copy-start.9
  350.6 1.5 copy-start.27
  356.8 2.9 copy-start.33
  482.6 6.3 copy-start.35
  484.3 0.8 copy-start.23
  487.2 0.8 copy-start.19
  587.1 14.3 %copy-start.22 = (f32[32,32,64]{2,1,0:T(8,128)S(1)}, f32[32,32,64]{2,1,0:T(8,128)}, u32[]{:S(2)}) copy-start(f32[32,32,64]{2,1,0:T(8,128)} %copy-done.21) | copy-start | bytes 786436
  587.2 14.3 %copy-start.32 = (f32[1,32,32,64]{3,2,1,0:T(8,128)S(1)}, f32[1,32,32,64]{3,2,1,0:T(8,128)}, u32[]{:S(2)}) copy-start(f32[1,32,32,64]{3,2,1,0:T(8,128)} %convolution_bitcast_fusion.10) | copy-start | bytes 786436
  600.8 2.4 copy-start.24
  601.4 2.4 copy-start.20
  603.2 1.3 copy-start.34
  607.9 2.0 copy-start.13
  607.9 2.0 copy-start.28
  608.9 2.1 copy-start.10
  609.9 7.4 %copy-start.29 = (f32[32,32,64]{2,1,0:T(8,128)}, f32[32,32,64]{2,1,0:T(8,128)S(1)}, u32[]{:S(2)}) copy-start(f32[32,32,64]{2,1,0:T(8,128)S(1)} %fusion.72) | copy-start | bytes 786436
  610.0 2.1 copy-start.18
  611.0 2.0 copy-start.4
  613.0 4.3 copy-start.31
  614.1 2.3 copy-start.7
  615.3 2.1 copy-start.26
  617.3 2.0 copy-start.37
  619.3 2.9 copy-start.15
  622.2 26.0 %copy-start.1 = (bf16[128,2048]{1,0:T(8,128)(2,1)S(1)}, bf16[128,2048]{1,0:T(8,128)(2,1)}, u32[]{:S(2)}) copy-start(bf16[128,2048]{1,0:T(8,128)(2,1)} %param.11) | copy-start | bytes 1572868
where the time goes:
time: 655 us; the launch traced here: 648 us
  other arithmetic  466 us (71%)
  matrix products  63.8 us (10%)
  blocking collectives  47.7 us (7%)
  local copies, waits for them, and re-layouts  42.2 us (6%)
  starting transfers between devices  18.5 us (3%)
  waiting for transfers between devices  8.81 us (1%)
    another operation x13, other arithmetic, factor_solve(): pivot_factor = jnp.linalg.cholesky(pivot)  381 us
    another operation x9, other arithmetic, factor_solve(): jax.scipy.linalg.solve_triangular(pivot_factor, identity, lower=True)  59.9 us
    all_gather x2, blocking collectives, prefix_2(): pieces = jax.tree.map(lambda part: lax.all_gather(part, axis), value)  28.6 us
    dot_general x16, matrix products, times_turned(): return jnp.einsum('...ij,...kj->...ik', left, right, precision=highest)  26.2 us
    all_to_all x1, blocking collectives, body(): lax.all_to_all(result, 'head', split_axis=0, concat_axis=1, tiled=True)  19 us
  transfers between devices with their start and end apart: 3, of which 1 were waited for; matrix products, arithmetic and copies ran while one was open for 43% of the time, Pallas kernels for 0%

commit v1 on v0

v1 whole, which is shorter than its diff:
```python
import jax
import jax.numpy as jnp
from jax import lax
from jax.experimental import pallas as pl
from jax.experimental.pallas import tpu as pltpu
from jax.sharding import PartitionSpec as P

HEADS = 16
DK = 128
GROUP = 64
ROWS = 128
SOURCES = 16
GROUPS = SOURCES * ROWS // GROUP
EDGE = 32
LEVELS = DK // EDGE
PACK = DK // EDGE

f32, bf16 = jnp.float32, jnp.bfloat16
epsilon = 1e-06


def lanes(shape):
    return lax.broadcasted_iota(jnp.int32, shape, len(shape) - 1)


def unit_rows(values):
    values_f = values.astype(f32)
    scale_back = lax.rsqrt(jnp.sum(values_f * values_f, axis=-1, keepdims=True) + epsilon)
    return (values_f * scale_back).astype(bf16)


def unit_kernel(q_ref, k_ref, v_ref, out_ref):
    for h in range(HEADS):
        columns = slice(h * DK, (h + 1) * DK)
        out_ref[h, :ROWS, :] = unit_rows(q_ref[:, columns])
        out_ref[h, ROWS : 2 * ROWS, :] = unit_rows(k_ref[:, columns])
        out_ref[h, 2 * ROWS :, :] = v_ref[:, columns]


def total_kernel(qkv_ref, out_ref):
    def add(source, total):
        k = qkv_ref[source, ROWS : 2 * ROWS, :]
        v = qkv_ref[source, 2 * ROWS :, :]
        return total + turned_dot(k, jnp.concatenate([k, v], axis=1))

    out_ref[...] = lax.fori_loop(0, SOURCES, add, jnp.zeros((DK, 2 * DK), f32), unroll=True)


def turned_dot(left, right):
    return lax.dot_general(left, right, (((0,), (0,)), ((), ())), preferred_element_type=f32)


def dot(left, right):
    return jnp.dot(left, right, preferred_element_type=f32)


def spread(x, quarter):
    x = jnp.where(lanes(x.shape) // EDGE == quarter, x, 0.0)
    x = x + pltpu.roll(x, EDGE, 1)
    return x + pltpu.roll(x, 2 * EDGE, 1)


def left_parts(x):
    lane = lanes(x.shape)
    rest = x - x.astype(bf16).astype(f32)
    low = rest - rest.astype(bf16).astype(f32)
    first = jnp.where(lane < 3 * EDGE, x, rest).astype(bf16)
    second = jnp.where(lane < 2 * EDGE, rest, low).astype(bf16)
    return jnp.concatenate([first, second], axis=1)


def right_parts(x):
    high = x.astype(bf16)
    rest = x - high.astype(f32)
    middle = rest.astype(bf16)
    low = (rest - middle.astype(f32)).astype(bf16)
    return jnp.concatenate([high, middle, low, high, middle, low, high, middle], axis=0)


def two_parts(x):
    high = x.astype(bf16)
    return high, (x - high.astype(f32)).astype(bf16)


def invert(rows):
    lane = lanes((8, DK)) % EDGE
    base = lanes((8, DK)) - lane
    for j in range(EDGE):
        here = lane == j

        def pick(x):
            return jnp.take_along_axis(x, base + j, axis=1)

        inverse = 1.0 / pick(rows[j])
        pivot = jnp.where(here, inverse, rows[j] * inverse)
        for r in range(EDGE):
            if r != j:
                rows[r] = jnp.where(here, 0.0, rows[r]) - pick(rows[r]) * pivot
        rows[j] = pivot
    return rows


def solve_kernel(mine_ref, qkv_ref, totals_ref, ridge_ref, out_ref, work, vk_start, running, packed):
    mine = mine_ref[0]
    row = lax.broadcasted_iota(jnp.int32, (DK, DK), 0)
    diagonal = jnp.where(row == lanes((DK, DK)), jnp.broadcast_to(ridge_ref[...], (DK, DK)), 0.0)
    start = jnp.concatenate([diagonal, jnp.zeros((DK, DK), f32)], axis=1)
    for i in range(totals_ref.shape[0] - 1):
        start = start + jnp.where(i < mine, 1.0, 0.0) * totals_ref[i]
    running[...] = start

    def fill(source, _):
        for half in range(ROWS // GROUP):
            c = source * (ROWS // GROUP) + half
            now = running[...]
            first = half * GROUP
            q = qkv_ref[source, first : first + GROUP, :]
            k = qkv_ref[source, ROWS + first : ROWS + first + GROUP, :]
            v = qkv_ref[source, 2 * ROWS + first : 2 * ROWS + first + GROUP, :]
            work[c, :DK, :] = now[:, :DK]
            work[c, DK:, :] = q.astype(f32)
            vk_start[c] = now[:, DK:]
            running[...] = now + turned_dot(k, jnp.concatenate([k, v], axis=1))
        return 0

    lax.fori_loop(0, SOURCES, fill, 0)

    for level in range(LEVELS):
        at = level * EDGE

        for s in range(GROUPS // PACK):
            tile = None
            for part in range(PACK):
                block = work[s * PACK + part, at : at + EDGE, :]
                if part != level:
                    block = pltpu.roll(block, (EDGE * (part - level)) % DK, 1)
                tile = block if part == 0 else jnp.where(lanes(block.shape) // EDGE == part, block, tile)
            packed[pl.ds(s, EDGE, stride=8), :] = tile
        rows = invert([packed[8 * r : 8 * r + 8, :] for r in range(EDGE)])
        for r in range(EDGE):
            packed[8 * r : 8 * r + 8, :] = rows[r]

        first = at + EDGE

        def eliminate(s, _):
            tile = packed[pl.ds(s, EDGE, stride=8), :]
            for part in range(PACK):
                c = s * PACK + part
                inverse = spread(tile, part)
                panel = dot(left_parts(inverse), right_parts(work[c, at:first, :]))
                panel = jnp.where(lanes(panel.shape) // EDGE == level, -inverse, panel)
                below = work[c, first:, :]
                change = dot(left_parts(spread(below, level)), right_parts(panel))
                work[c, first:, :] = jnp.where(lanes(below.shape) // EDGE == level, 0.0, below) - change
            return 0

        lax.fori_loop(0, GROUPS // PACK, eliminate, 0)

    def apply(source, _):
        for half in range(ROWS // GROUP):
            c = source * (ROWS // GROUP) + half
            first = half * GROUP
            k = qkv_ref[source, ROWS + first : ROWS + first + GROUP, :]
            v = qkv_ref[source, 2 * ROWS + first : 2 * ROWS + first + GROUP, :]
            high, low = two_parts(work[c, DK:, :])
            vk_high, vk_low = two_parts(vk_start[c])
            mixed = dot(jnp.concatenate([high, high], axis=1), jnp.concatenate([vk_high, vk_low], axis=0))
            mixed = mixed + dot(low, vk_high)
            scores = lax.dot_general(
                jnp.concatenate([high, low], axis=1),
                jnp.concatenate([k, k], axis=1),
                (((1,), (1,)), ((), ())),
                preferred_element_type=f32,
            )
            causal = lanes((GROUP, GROUP)) <= lax.broadcasted_iota(jnp.int32, (GROUP, GROUP), 0)
            high, low = two_parts(jnp.where(causal, scores, 0.0))
            mixed = mixed + dot(high, v) + dot(low, v)
            out_ref[source, first : first + GROUP, :] = mixed.astype(bf16)
        return 0

    lax.fori_loop(0, SOURCES, apply, 0)


def whole():
    return pl.BlockSpec(memory_space=pltpu.VMEM)


def body(queries, key_rows, value_rows, ridge_diag):
    parts = pl.pallas_call(
        unit_kernel,
        out_shape=jax.ShapeDtypeStruct((HEADS, 3 * ROWS, DK), bf16),
        in_specs=[whole()] * 3,
        out_specs=whole(),
        name="unit",
    )(queries, key_rows, value_rows)
    parts = lax.all_to_all(parts, "head", split_axis=0, concat_axis=0, tiled=True)
    total = pl.pallas_call(
        total_kernel,
        out_shape=jax.ShapeDtypeStruct((DK, 2 * DK), f32),
        in_specs=[whole()],
        out_specs=whole(),
        name="total",
    )(parts)
    totals = lax.all_gather(total, "seq")
    ridge_here = lax.dynamic_slice_in_dim(ridge_diag, lax.axis_index("head"), 1, 0)
    mine = lax.axis_index("seq").astype(jnp.int32).reshape(1)
    mixed = pl.pallas_call(
        solve_kernel,
        out_shape=jax.ShapeDtypeStruct((SOURCES, ROWS, DK), bf16),
        in_specs=[pl.BlockSpec(memory_space=pltpu.SMEM)] + [whole()] * 3,
        out_specs=whole(),
        scratch_shapes=[
            pltpu.VMEM((GROUPS, DK + GROUP, DK), f32),
            pltpu.VMEM((GROUPS, DK, DK), f32),
            pltpu.VMEM((DK, 2 * DK), f32),
            pltpu.VMEM((EDGE * 8, DK), f32),
        ],
        compiler_params=pltpu.CompilerParams(vmem_limit_bytes=40 * 2**20),
        name="solve",
    )(mine, parts, totals, ridge_here)
    mixed = lax.all_to_all(mixed, "head", split_axis=0, concat_axis=0, tiled=True)
    return jnp.transpose(mixed, (1, 0, 2)).reshape(ROWS, HEADS * DK)


def solution(mesh):
    in_specs = (P(("seq", "head"), None), P(("seq", "head"), None), P(("seq", "head"), None), P())
    out_specs = P(("seq", "head"), None)
    return jax.shard_map(body, mesh=mesh, in_specs=in_specs, out_specs=out_specs, check_vma=False)
```

time: 655 us -> 133 us (0.20)
  other arithmetic: 466 us -> 0 us
  matrix products: 63.8 us -> 0 us
  Pallas kernels: 0 us -> 46.1 us
  local copies, waits for them, and re-layouts: 42.2 us -> 2.57 us
  starting transfers between devices: 18.5 us -> 0.01 us
  waiting for transfers between devices: 8.81 us -> 22.2 us
  between operations: 1.19 us -> 13.4 us
    another operation x24 -> x0, other arithmetic: 446 us -> none  [the longest x13 381 us: factor_solve(): pivot_factor = jnp.linalg.cholesky(pivot)]
    dot_general x41 -> x0, matrix products: 59.3 us -> none  [the longest x16 26.2 us: times_turned(): return jnp.einsum('...ij,...kj->...ik', left, right, precision=highest)]
    pallas_call x0 -> x3, Pallas kernels: none -> 46.1 us  [the longest x1 40.3 us: body(): pl.pallas_call(solve_kernel, out_shape=jax.ShapeDtypeStruct((SOURCES, ROW...]
    all_to_all x1 -> x2, blocking collectives: 19 us -> 48.6 us  [the longest x1 30 us: body(): lax.all_to_all(parts, 'head', split_axis=0, concat_axis=0, tiled=True)]
    all_gather x2 -> x0, blocking collectives: 28.6 us -> none  [prefix_2(): pieces = jax.tree.map(lambda part: lax.all_gather(part, axis), value)]
    all_gather x0 -> x1, waiting for transfers between devices: none -> 22.2 us  [body(): totals = lax.all_gather(total, 'seq')]
    all_to_all x3 -> x0, starting transfers between devices: 18.5 us -> none  [the longest x1 7.15 us: body(): lax.all_to_all(queries, 'head', split_axis=1, concat_axis=0, tiled=True)]
    another operation x10 -> x0, local copies, waits for them, and re-layouts: 17.9 us -> none  [the longest x4 5.92 us: factor_solve(): pivot_factor = jnp.linalg.cholesky(pivot)]
  transfers between devices with their start and end apart: 3 -> 1, of which waited for: 1 -> 1; matrix products, arithmetic and copies ran while one was open for 43% -> 0% of each run, Pallas kernels for 0% -> 0%
where the time goes in v1:
time: 133 us
  blocking collectives  48.6 us (37%)
  Pallas kernels  46.1 us (35%)
  waiting for transfers between devices  22.2 us (17%)
  between operations  13.4 us (10%)
  local copies, waits for them, and re-layouts  2.57 us (2%)
    pallas_call x1, Pallas kernels, body(): pl.pallas_call(solve_kernel, out_shape=jax.ShapeDtypeStruct((SOURCES, ROW...  40.3 us
    all_to_all x1, blocking collectives, body(): lax.all_to_all(parts, 'head', split_axis=0, concat_axis=0, tiled=True)  30 us
    all_gather x1, waiting for transfers between devices, body(): totals = lax.all_gather(total, 'seq')  22.2 us
    all_to_all x1, blocking collectives, body(): lax.all_to_all(mixed, 'head', split_axis=0, concat_axis=0, tiled=True)  18.6 us
    pallas_call x1, Pallas kernels, body(): pl.pallas_call(unit_kernel, out_shape=jax.ShapeDtypeStruct((HEADS, 3 * RO...  3.18 us
  transfers between devices with their start and end apart: 1, of which 1 were waited for; matrix products, arithmetic and copies ran while one was open for 0% of the time, Pallas kernels for 0%

profile of v1, /device:TPU:0, one launch (start us, length us, event | category | flops | bytes accessed | tf_op | source)
XLA Modules:
  0.0 132.9 jit_solution(2215427924637793744)
XLA Ops:
  6.5 0.0 copy-start
  6.5 0.0 all-gather.3.cloned.1.call-start
  6.5 3.2 %unit.1 = bf16[16,384,128]{2,1,0:T(8,128)(2,1)} custom-call(bf16[128,2048]{1,0:T(8,128)(2,1)} %q_ref.1, bf16[128,2048]{1,0:T(8,128)(2,1)} %k_ref.1, bf16[128,2048]{1,0:T(8,128)(2,1)} %v_ref.1), custom_call_target="tpu_custom_call" | custom-call | tf_op jit(solution)/shard_map/unit/pallas_call | solution.py:189
  9.7 30.0 %all_to_all.10.qkv_ref = bf16[16,384,128]{2,1,0:T(8,128)(2,1)} all-to-all(bf16[16,384,128]{2,1,0:T(8,128)(2,1)} %unit.1), channel_id=1, replica_groups=mesh['seq'=8,'head'=16] {'head'}, dimensions={0} | all-to-all | bytes 3145728 | tf_op jit(solution)/shard_map/all_to_all | solution.py:196
  39.7 0.0 copy-start.1
  39.7 2.6 %total.1 = f32[128,256]{1,0:T(8,128)} custom-call(bf16[16,384,128]{2,1,0:T(8,128)(2,1)} %all_to_all.10.qkv_ref), custom_call_target="tpu_custom_call" | custom-call | tf_op jit(solution)/shard_map/total/pallas_call | solution.py:197
  42.4 0.0 all-gather.3.cloned.1.call-update
  42.4 0.0 copy-done
  42.4 22.2 %all-gather.3.cloned.1.call-done = f32[1024,256]{1,0:T(8,128)} async-done(((f32[128,256]{1,0:T(8,128)}), f32[1024,256]{1,0:T(8,128)}) %all-gather.3.cloned.1.call-update) | async-done | bytes 1048592 | tf_op jit(solution)/shard_map/all_gather | solution.py:204
  64.6 0.0 copy-done.1
  64.6 0.0 copy-start.2
  64.6 1.2 copy-done.2
  65.8 40.3 %solve.1 = bf16[16,128,128]{2,1,0:T(8,128)(2,1)S(1)} custom-call(s32[1]{0:T(128)} %bitcast.mine_ref, bf16[16,384,128]{2,1,0:T(8,128)(2,1)S(1)} %copy-done.1, f32[8,128,256]{2,1,0:T(8,128)S(1)} %bitcast.4, f32[1,128]{1,0:T(1,128)S(1)} %constant_dynamic-slice_fusion.ridge_ref), custom_call_target="tpu_custom_call" | custom-call | tf_op jit(solution)/shard_map/solve/pallas_call | solution.py:207
  106.1 18.6 %all_to_all.11 = bf16[16,128,128]{2,1,0:T(8,128)(2,1)S(1)} all-to-all(bf16[16,128,128]{2,1,0:T(8,128)(2,1)S(1)} %solve.1), channel_id=1, replica_groups=mesh['seq'=8,'head'=16] {'head'}, dimensions={0} | all-to-all | bytes 1048576 | tf_op jit(solution)/shard_map/all_to_all | solution.py:221
  124.7 0.3 copy.5
  125.0 1.0 copy.6
  (1 shorter events, 0.0 us)
Async XLA Ops:
  6.5 35.9 %copy-start = (f32[16,128]{1,0:T(8,128)S(1)}, f32[16,128]{1,0:T(8,128)}, u32[]{:S(2)}) copy-start(f32[16,128]{1,0:T(8,128)} %param.7) | copy-start | bytes 24580
  6.5 58.1 %all-gather.3.cloned.1.call-start = ((), (), s32[]{:S(2)}) async-start(), calls=%async_computation.2 | async-start | bytes 1179648 | tf_op jit(solution)/shard_map/all_gather | solution.py:204
  39.7 24.9 %copy-start.1 = (bf16[16,384,128]{2,1,0:T(8,128)(2,1)S(1)}, bf16[16,384,128]{2,1,0:T(8,128)(2,1)}, u32[]{:S(2)}) copy-start(bf16[16,384,128]{2,1,0:T(8,128)(2,1)} %all_to_all.10.qkv_ref) | copy-start | bytes 4718596
  64.6 1.2 copy-start.2
Sparse Core Ops, SparseCore 0:
  42.5 22.0 all-gather.2

commit v2 on v1

v2 whole, which is shorter than its diff:
```python
import jax
import jax.numpy as jnp
from jax import lax
from jax.experimental import pallas as pl
from jax.experimental.pallas import tpu as pltpu
from jax.sharding import PartitionSpec as P

HEADS = 16
DK = 128
GROUP = 64
ROWS = 128
SOURCES = 16
GROUPS = SOURCES * ROWS // GROUP
EDGE = 32
LEVELS = DK // EDGE
PACK = DK // EDGE

f32, bf16 = jnp.float32, jnp.bfloat16
epsilon = 1e-06


def lanes(shape):
    return lax.broadcasted_iota(jnp.int32, shape, len(shape) - 1)


def unit_rows(values):
    values_f = values.astype(f32)
    scale_back = lax.rsqrt(jnp.sum(values_f * values_f, axis=-1, keepdims=True) + epsilon)
    return (values_f * scale_back).astype(bf16)


def unit_kv_kernel(k_ref, v_ref, out_ref):
    for h in range(HEADS):
        columns = slice(h * DK, (h + 1) * DK)
        out_ref[h, :ROWS, :] = unit_rows(k_ref[:, columns])
        out_ref[h, ROWS:, :] = v_ref[:, columns]


def unit_q_kernel(q_ref, out_ref):
    for h in range(HEADS):
        out_ref[h] = unit_rows(q_ref[:, h * DK : (h + 1) * DK])


def total_kernel(kv_ref, out_ref):
    def add(source, total):
        k = kv_ref[source, :ROWS, :]
        v = kv_ref[source, ROWS:, :]
        return total + turned_dot(k, jnp.concatenate([k, v], axis=1))

    out_ref[...] = lax.fori_loop(0, SOURCES, add, jnp.zeros((DK, 2 * DK), f32), unroll=True)


def token_kernel(mixed_ref, out_ref):
    for h in range(HEADS):
        out_ref[:, h * DK : (h + 1) * DK] = mixed_ref[h]


def turned_dot(left, right):
    return lax.dot_general(left, right, (((0,), (0,)), ((), ())), preferred_element_type=f32)


def dot(left, right):
    return jnp.dot(left, right, preferred_element_type=f32)


def spread(x, quarter):
    return jnp.take_along_axis(x, quarter * EDGE + lanes(x.shape) % EDGE, axis=1)


def left_parts(x):
    lane = lanes(x.shape)
    rest = x - x.astype(bf16).astype(f32)
    low = rest - rest.astype(bf16).astype(f32)
    first = jnp.where(lane < 3 * EDGE, x, rest).astype(bf16)
    second = jnp.where(lane < 2 * EDGE, rest, low).astype(bf16)
    return jnp.concatenate([first, second], axis=1)


def right_parts(x):
    high = x.astype(bf16)
    rest = x - high.astype(f32)
    middle = rest.astype(bf16)
    low = (rest - middle.astype(f32)).astype(bf16)
    return jnp.concatenate([high, middle, low, high, middle, low, high, middle], axis=0)


def two_parts(x):
    high = x.astype(bf16)
    return high, (x - high.astype(f32)).astype(bf16)


def invert(rows):
    lane = lanes((8, DK)) % EDGE
    base = lanes((8, DK)) - lane

    def pick(x, j):
        return jnp.take_along_axis(x, base + j, axis=1)

    for j in range(0, EDGE, 2):
        first, second = rows[j], rows[j + 1]
        a, b, d = pick(first, j), pick(first, j + 1), pick(second, j + 1)
        scale = 1.0 / (a * d - b * b)
        a, b, d = a * scale, b * scale, d * scale
        at_first, at_second = lane == j, lane == j + 1
        pivot_first = jnp.where(at_first, d, jnp.where(at_second, -b, d * first - b * second))
        pivot_second = jnp.where(at_first, -b, jnp.where(at_second, a, a * second - b * first))
        for r in [*range(j + 2, EDGE), *range(j)]:
            x = rows[r]
            kept = jnp.where(at_first | at_second, 0.0, x)
            rows[r] = kept - pick(x, j) * pivot_first - pick(x, j + 1) * pivot_second
        rows[j], rows[j + 1] = pivot_first, pivot_second
    return rows


def solve_kernel(odd_ref, q_ref, kv_ref, one_ref, two_ref, three_ref, partner_ref, ridge_ref, out_ref, work_even, work_odd, vk_start, packed):
    row = lax.broadcasted_iota(jnp.int32, (DK, DK), 0)
    diagonal = jnp.where(row == lanes((DK, DK)), jnp.broadcast_to(ridge_ref[...], (DK, DK)), 0.0)
    start = one_ref[...] + two_ref[...] + three_ref[...]
    start = start + jnp.where(odd_ref[0] == 1, partner_ref[...], 0.0)
    work_even[0, :DK, :] = start[:, :DK] + diagonal
    vk_start[0] = start[:, DK:]

    def fill(source, _):
        for half in range(ROWS // GROUP):
            c = source * (ROWS // GROUP) + half
            first = half * GROUP
            k = kv_ref[source, first : first + GROUP, :]
            v = kv_ref[source, ROWS + first : ROWS + first + GROUP, :]
            work_even[c, DK:, :] = q_ref[source, first : first + GROUP, :].astype(f32)
            group = turned_dot(k, jnp.concatenate([k, v], axis=1))
            work_even[c + 1, :DK, :] = work_even[c, :DK, :] + group[:, :DK]
            vk_start[c + 1] = vk_start[c] + group[:, DK:]
        return 0

    lax.fori_loop(0, SOURCES, fill, 0, unroll=2)

    work = (work_even, work_odd)
    for level in range(LEVELS):
        before, after = work[level % 2], work[1 - level % 2]
        at = level * EDGE
        first = at + EDGE

        for s in range(GROUPS // PACK):
            tile = None
            for part in range(PACK):
                block = before[s * PACK + part, at:first, :]
                if part != level:
                    block = pltpu.roll(block, (EDGE * (part - level)) % DK, 1)
                tile = block if part == 0 else jnp.where(lanes(block.shape) // EDGE == part, block, tile)
            packed[pl.ds(s, EDGE, stride=8), :] = tile
        rows = invert([packed[8 * r : 8 * r + 8, :] for r in range(EDGE)])
        for r in range(EDGE):
            packed[8 * r : 8 * r + 8, :] = rows[r]

        def eliminate(s, _):
            tile = packed[pl.ds(s, EDGE, stride=8), :]
            for part in range(PACK):
                c = s * PACK + part
                inverse = spread(tile, part)
                panel = dot(left_parts(inverse), right_parts(before[c, at:first, :]))
                panel = jnp.where(lanes(panel.shape) // EDGE == level, -inverse, panel)
                below = before[c, first:, :]
                change = dot(left_parts(spread(below, level)), right_parts(panel))
                after[c, first:, :] = jnp.where(lanes(below.shape) // EDGE == level, 0.0, below) - change
            return 0

        lax.fori_loop(0, GROUPS // PACK, eliminate, 0, unroll=2)

    def apply(source, _):
        for half in range(ROWS // GROUP):
            c = source * (ROWS // GROUP) + half
            first = half * GROUP
            k = kv_ref[source, first : first + GROUP, :]
            v = kv_ref[source, ROWS + first : ROWS + first + GROUP, :]
            high, low = two_parts(work_even[c, DK:, :])
            vk_high, vk_low = two_parts(vk_start[c])
            mixed = dot(jnp.concatenate([high, high], axis=1), jnp.concatenate([vk_high, vk_low], axis=0))
            mixed = mixed + dot(low, vk_high)
            scores = lax.dot_general(
                jnp.concatenate([high, low], axis=1),
                jnp.concatenate([k, k], axis=1),
                (((1,), (1,)), ((), ())),
                preferred_element_type=f32,
            )
            causal = lanes((GROUP, GROUP)) <= lax.broadcasted_iota(jnp.int32, (GROUP, GROUP), 0)
            high, low = two_parts(jnp.where(causal, scores, 0.0))
            mixed = mixed + dot(high, v) + dot(low, v)
            out_ref[source, first : first + GROUP, :] = mixed.astype(bf16)
        return 0

    lax.fori_loop(0, SOURCES, apply, 0, unroll=2)


def whole():
    return pl.BlockSpec(memory_space=pltpu.VMEM)


def body(queries, key_rows, value_rows, ridge_diag):
    seq = lax.axis_size("seq")
    kv = pl.pallas_call(
        unit_kv_kernel,
        out_shape=jax.ShapeDtypeStruct((HEADS, 2 * ROWS, DK), bf16),
        in_specs=[whole()] * 2,
        out_specs=whole(),
        compiler_params=pltpu.CompilerParams(vmem_limit_bytes=6 * 2**20),
        name="unit_kv",
    )(key_rows, value_rows)
    kv = lax.all_to_all(kv, "head", split_axis=0, concat_axis=0, tiled=True)
    q = pl.pallas_call(
        unit_q_kernel,
        out_shape=jax.ShapeDtypeStruct((HEADS, ROWS, DK), bf16),
        in_specs=[whole()],
        out_specs=whole(),
        compiler_params=pltpu.CompilerParams(vmem_limit_bytes=6 * 2**20),
        name="unit_q",
    )(queries)
    q = lax.all_to_all(q, "head", split_axis=0, concat_axis=0, tiled=True)
    total = pl.pallas_call(
        total_kernel,
        out_shape=jax.ShapeDtypeStruct((DK, 2 * DK), f32),
        in_specs=[whole()],
        out_specs=whole(),
        compiler_params=pltpu.CompilerParams(vmem_limit_bytes=6 * 2**20),
        name="total",
    )(kv)
    partner = lax.ppermute(total, "seq", [(i, i ^ 1) for i in range(seq)])
    chip = total + partner
    earlier = [
        lax.ppermute(chip, "seq", [(i, i + step) for i in range(seq - step)]) for step in range(2, seq, 2)
    ]
    ridge_here = lax.dynamic_slice_in_dim(ridge_diag, lax.axis_index("head"), 1, 0)
    odd = (lax.axis_index("seq") % 2).astype(jnp.int32).reshape(1)
    mixed = pl.pallas_call(
        solve_kernel,
        out_shape=jax.ShapeDtypeStruct((SOURCES, ROWS, DK), bf16),
        in_specs=[pl.BlockSpec(memory_space=pltpu.SMEM)] + [whole()] * 7,
        out_specs=whole(),
        scratch_shapes=[
            pltpu.VMEM((GROUPS + 1, DK + GROUP, DK), f32),
            pltpu.VMEM((GROUPS, DK + GROUP, DK), f32),
            pltpu.VMEM((GROUPS + 1, DK, DK), f32),
            pltpu.VMEM((EDGE * 8, DK), f32),
        ],
        compiler_params=pltpu.CompilerParams(vmem_limit_bytes=16 * 2**20),
        name="solve",
    )(odd, q, kv, *earlier, partner, ridge_here)
    mixed = lax.all_to_all(mixed, "head", split_axis=0, concat_axis=0, tiled=True)
    return pl.pallas_call(
        token_kernel,
        out_shape=jax.ShapeDtypeStruct((ROWS, HEADS * DK), bf16),
        in_specs=[whole()],
        out_specs=whole(),
        compiler_params=pltpu.CompilerParams(vmem_limit_bytes=6 * 2**20),
        name="to_tokens",
    )(mixed)


def solution(mesh):
    in_specs = (P(("seq", "head"), None), P(("seq", "head"), None), P(("seq", "head"), None), P())
    out_specs = P(("seq", "head"), None)
    return jax.shard_map(body, mesh=mesh, in_specs=in_specs, out_specs=out_specs, check_vma=False)
```

time: 133 us -> 93.3 us (0.70)
  blocking collectives: 48.6 us -> 18 us
  starting transfers between devices: 0.01 us -> 20.9 us
  Pallas kernels: 46.1 us -> 30.1 us
  between operations: 13.4 us -> 0.11 us
  waiting for transfers between devices: 22.2 us -> 20.8 us
    all_to_all x1 -> x0, blocking collectives: 30 us -> none  [body(): lax.all_to_all(parts, 'head', split_axis=0, concat_axis=0, tiled=True)]
    all_gather x1 -> x0, waiting for transfers between devices: 22.2 us -> none  [body(): totals = lax.all_gather(total, 'seq')]
    all_to_all x0 -> x2, waiting for transfers between devices: none -> 16.5 us  [the longest x1 16.5 us: body(): kv = lax.all_to_all(kv, 'head', split_axis=0, concat_axis=0, tiled=True)]
    pallas_call x1, Pallas kernels: 40.3 us -> 26.2 us  [body(): pl.pallas_call(solve_kernel, out_shape=jax.ShapeDtypeStruct((SOURCES, ROW...]
    all_to_all x0 -> x2, starting transfers between devices: none -> 10.8 us  [the longest x1 7.25 us: body(): kv = lax.all_to_all(kv, 'head', split_axis=0, concat_axis=0, tiled=True)]
    ppermute x0 -> x4, starting transfers between devices: none -> 10.1 us  [the longest x3 10 us: body(): lax.ppermute(chip, 'seq', [(i, i + step) for i in range(seq - step)])]
    ppermute x0 -> x4, waiting for transfers between devices: none -> 4.37 us  [the longest x3 3.03 us: body(): lax.ppermute(chip, 'seq', [(i, i + step) for i in range(seq - step)])]
    pallas_call x1, Pallas kernels: 2.65 us -> 0.46 us  [body(): pl.pallas_call(total_kernel, out_shape=jax.ShapeDtypeStruct((DK, 2 * DK),...]
  transfers between devices with their start and end apart: 1 -> 6, of which waited for: 1 -> 4; matrix products, arithmetic and copies ran while one was open for 0% -> 0% of each run, Pallas kernels for 0% -> 2%
where the time goes in v2:
time: 93.3 us; the launch traced here: 92.1 us
  Pallas kernels  30.1 us (32%)
  starting transfers between devices  20.9 us (22%)
  waiting for transfers between devices  20.8 us (22%)
  blocking collectives  18 us (19%)
  local copies, waits for them, and re-layouts  2.11 us (2%)
    pallas_call x1, Pallas kernels, body(): pl.pallas_call(solve_kernel, out_shape=jax.ShapeDtypeStruct((SOURCES, ROW...  26.2 us
    all_to_all x1, blocking collectives, body(): lax.all_to_all(mixed, 'head', split_axis=0, concat_axis=0, tiled=True)  18 us
    all_to_all x1, waiting for transfers between devices, body(): kv = lax.all_to_all(kv, 'head', split_axis=0, concat_axis=0, tiled=True)  16.5 us
    ppermute x3, starting transfers between devices, body(): lax.ppermute(chip, 'seq', [(i, i + step) for i in range(seq - step)])  10 us
    all_to_all x1, starting transfers between devices, body(): kv = lax.all_to_all(kv, 'head', split_axis=0, concat_axis=0, tiled=True)  7.25 us
    all_to_all x1, starting transfers between devices, body(): q = lax.all_to_all(q, 'head', split_axis=0, concat_axis=0, tiled=True)  3.57 us
    ppermute x3, waiting for transfers between devices, body(): lax.ppermute(chip, 'seq', [(i, i + step) for i in range(seq - step)])  3.03 us
    unnamed x8, local copies, waits for them, and re-layouts  2.1 us
  transfers between devices with their start and end apart: 6, of which 4 were waited for; matrix products, arithmetic and copies ran while one was open for 0% of the time, Pallas kernels for 2%

profile of v2, /device:TPU:0, one launch (start us, length us, event | category | flops | bytes accessed | tf_op | source)
XLA Modules:
  0.0 92.1 jit_solution(4726495982722433001)
XLA Ops:
  0.0 0.0 copy-start
  0.0 0.0 copy-start.2
  0.0 1.1 %copy-done.2 = bf16[128,2048]{1,0:T(8,128)(2,1)S(1)} copy-done((bf16[128,2048]{1,0:T(8,128)(2,1)S(1)}, bf16[128,2048]{1,0:T(8,128)(2,1)}, u32[]{:S(2)}) %copy-start.2) | copy-done | bytes 524312
  1.1 0.0 copy-start.3
  1.1 1.0 %copy-done.3 = bf16[128,2048]{1,0:T(8,128)(2,1)S(1)} copy-done((bf16[128,2048]{1,0:T(8,128)(2,1)S(1)}, bf16[128,2048]{1,0:T(8,128)(2,1)}, u32[]{:S(2)}) %copy-start.3) | copy-done | bytes 524312
  2.1 1.4 %unit_kv.1 = bf16[16,256,128]{2,1,0:T(8,128)(2,1)} custom-call(bf16[128,2048]{1,0:T(8,128)(2,1)S(1)} %copy-done.2, bf16[128,2048]{1,0:T(8,128)(2,1)S(1)} %copy-done.3), custom_call_target="tpu_custom_call" | custom-call | tf_op jit(solution)/shard_map/unit_kv/pallas_call | solution.py:200
  3.5 0.0 copy-start.1
  3.5 7.2 %all-to-all-start.1 = ((bf16[16,256,128]{2,1,0:T(8,128)(2,1)}), bf16[16,256,128]{2,1,0:T(8,128)(2,1)S(1)}, u32[]{:S(2)}, u32[]{:S(2)}) async-start(bf16[16,256,128]{2,1,0:T(8,128)(2,1)} %unit_kv.1), calls=%async_computation.1 | async-start | bytes 2097152 | tf_op jit(solution)/shard_map/all_to_all | solution.py:208
  10.7 0.0 copy-done.1
  10.7 1.2 %unit_q.1 = bf16[16,128,128]{2,1,0:T(8,128)(2,1)} custom-call(bf16[128,2048]{1,0:T(8,128)(2,1)S(1)} %copy-done.1), custom_call_target="tpu_custom_call" | custom-call | tf_op jit(solution)/shard_map/unit_q/pallas_call | solution.py:209
  11.9 16.5 %all-to-all-done.1.kv_ref = bf16[16,256,128]{2,1,0:T(8,128)(2,1)S(1)} async-done(((bf16[16,256,128]{2,1,0:T(8,128)(2,1)}), bf16[16,256,128]{2,1,0:T(8,128)(2,1)S(1)}, u32[]{:S(2)}, u32[]{:S(2)}) %all-to-all-start.1) | async-done | bytes 1048608 | tf_op jit(solution)/shard_map/all_to_all | solution.py:208
  28.4 3.6 %all-to-all-start = ((bf16[16,128,128]{2,1,0:T(8,128)(2,1)}), bf16[16,128,128]{2,1,0:T(8,128)(2,1)S(1)}, u32[]{:S(2)}, u32[]{:S(2)}) async-start(bf16[16,128,128]{2,1,0:T(8,128)(2,1)} %unit_q.1), calls=%async_computation | async-start | bytes 1048576 | tf_op jit(solution)/shard_map/all_to_all | solution.py:217
  32.0 0.5 total.1
  32.4 0.1 collective-permute-start
  32.5 1.3 %collective-permute-done.partner_ref = f32[128,256]{1,0:T(8,128)S(1)} collective-permute-done((f32[128,256]{1,0:T(8,128)S(1)}, f32[128,256]{1,0:T(8,128)S(1)}, u32[]{:S(2)}, u32[]{:S(2)}) %collective-permute-start) | collective-permute-done | bytes 131104 | tf_op jit(solution)/shard_map/ppermute | solution.py:226
  33.9 6.0 %collective-permute-start.3 = (f32[128,256]{1,0:T(8,128)S(1)}, f32[128,256]{1,0:T(8,128)S(1)}, u32[]{:S(2)}, u32[]{:S(2)}) collective-permute-start(f32[128,256]{1,0:T(8,128)S(1)} %add.11), channel_id=1, source_target_pairs={{0,96},{16,112},{1,97},{17,113},{2,98},{18,114},{3,99},{19,115},{4... | collective-permute-start | bytes 393224 | tf_op jit(solution)/shard_map/ppermute | solution.py:229
  39.8 1.3 %collective-permute-start.2 = (f32[128,256]{1,0:T(8,128)S(1)}, f32[128,256]{1,0:T(8,128)S(1)}, u32[]{:S(2)}, u32[]{:S(2)}) collective-permute-start(f32[128,256]{1,0:T(8,128)S(1)} %add.11), channel_id=1, source_target_pairs={{0,64},{16,80},{32,96},{48,112},{1,65},{17,81},{33,97},{49,113},{2... | collective-permute-start | bytes 393224 | tf_op jit(solution)/shard_map/ppermute | solution.py:229
  41.1 2.8 %collective-permute-start.1 = (f32[128,256]{1,0:T(8,128)S(1)}, f32[128,256]{1,0:T(8,128)S(1)}, u32[]{:S(2)}, u32[]{:S(2)}) collective-permute-start(f32[128,256]{1,0:T(8,128)S(1)} %add.11), channel_id=1, source_target_pairs={{0,32},{16,48},{32,64},{48,80},{64,96},{80,112},{1,33},{17,49},{33... | collective-permute-start | bytes 393224 | tf_op jit(solution)/shard_map/ppermute | solution.py:229
  43.9 0.0 copy-done
  43.9 0.0 all-to-all-done.q_ref
  44.0 1.8 %collective-permute-done.3.three_ref = f32[128,256]{1,0:T(8,128)S(1)} collective-permute-done((f32[128,256]{1,0:T(8,128)S(1)}, f32[128,256]{1,0:T(8,128)S(1)}, u32[]{:S(2)}, u32[]{:S(2)}) %collective-permute-start.3) | collective-permute-done | bytes 131104 | tf_op jit(solution)/shard_map/ppermute | solution.py:229
  45.7 0.0 collective-permute-done.2.two_ref
  45.7 1.3 %collective-permute-done.1.one_ref = f32[128,256]{1,0:T(8,128)S(1)} collective-permute-done((f32[128,256]{1,0:T(8,128)S(1)}, f32[128,256]{1,0:T(8,128)S(1)}, u32[]{:S(2)}, u32[]{:S(2)}) %collective-permute-start.1) | collective-permute-done | bytes 131104 | tf_op jit(solution)/shard_map/ppermute | solution.py:229
  47.0 26.2 %solve.1 = bf16[16,128,128]{2,1,0:T(8,128)(2,1)S(1)} custom-call(s32[1]{0:T(128)} %bitcast.odd_ref, bf16[16,128,128]{2,1,0:T(8,128)(2,1)S(1)} %all-to-all-done.q_ref, bf16[16,256,128]{2,1,0:T(8,128)(2,1)S(1)} %all-to-all-done.1.kv_ref, f32[128,256]{1,0:T(8,128)S(1)} %collective-permute-done.1.one_ref, f32[128,256]{1,0:T(8,128)S(1)} %collective-permute-done.2.two_ref, ...), custom_call_target="tpu_custom_call" | custom-call | tf_op jit(solution)/shard_map/solve/pallas_call | solution.py:233
  73.2 18.0 %all_to_all.15.mixed_ref = bf16[16,128,128]{2,1,0:T(8,128)(2,1)S(1)} all-to-all(bf16[16,128,128]{2,1,0:T(8,128)(2,1)S(1)} %solve.1), channel_id=1, replica_groups=mesh['seq'=8,'head'=16] {'head'}, dimensions={0} | all-to-all | bytes 1048576 | tf_op jit(solution)/shard_map/all_to_all | solution.py:247
  91.2 0.9 %to_tokens.1 = bf16[128,2048]{1,0:T(8,128)(2,1)} custom-call(bf16[16,128,128]{2,1,0:T(8,128)(2,1)S(1)} %all_to_all.15.mixed_ref), custom_call_target="tpu_custom_call" | custom-call | tf_op jit(solution)/shard_map/to_tokens/pallas_call | solution.py:248
  (2 shorter events, 0.0 us)
Async XLA Ops:
  0.0 43.9 %copy-start = (f32[16,128]{1,0:T(8,128)S(1)}, f32[16,128]{1,0:T(8,128)}, u32[]{:S(2)}) copy-start(f32[16,128]{1,0:T(8,128)} %param.7) | copy-start | bytes 24580
  0.0 1.1 %copy-start.2 = (bf16[128,2048]{1,0:T(8,128)(2,1)S(1)}, bf16[128,2048]{1,0:T(8,128)(2,1)}, u32[]{:S(2)}) copy-start(bf16[128,2048]{1,0:T(8,128)(2,1)} %k_ref.1) | copy-start | bytes 1572868
  1.1 1.0 %copy-start.3 = (bf16[128,2048]{1,0:T(8,128)(2,1)S(1)}, bf16[128,2048]{1,0:T(8,128)(2,1)}, u32[]{:S(2)}) copy-start(bf16[128,2048]{1,0:T(8,128)(2,1)} %v_ref.1) | copy-start | bytes 1572868
  3.5 7.3 %copy-start.1 = (bf16[128,2048]{1,0:T(8,128)(2,1)S(1)}, bf16[128,2048]{1,0:T(8,128)(2,1)}, u32[]{:S(2)}) copy-start(bf16[128,2048]{1,0:T(8,128)(2,1)} %q_ref.1) | copy-start | bytes 1572868
  3.5 24.9 %all-to-all-start.1 = ((bf16[16,256,128]{2,1,0:T(8,128)(2,1)}), bf16[16,256,128]{2,1,0:T(8,128)(2,1)S(1)}, u32[]{:S(2)}, u32[]{:S(2)}) async-start(bf16[16,256,128]{2,1,0:T(8,128)(2,1)} %unit_kv.1), calls=%async_computation.1 | async-start | bytes 2097152 | tf_op jit(solution)/shard_map/all_to_all | solution.py:208
  28.4 15.6 %all-to-all-start = ((bf16[16,128,128]{2,1,0:T(8,128)(2,1)}), bf16[16,128,128]{2,1,0:T(8,128)(2,1)S(1)}, u32[]{:S(2)}, u32[]{:S(2)}) async-start(bf16[16,128,128]{2,1,0:T(8,128)(2,1)} %unit_q.1), calls=%async_computation | async-start | bytes 1048576 | tf_op jit(solution)/shard_map/all_to_all | solution.py:217
  32.4 1.4 %collective-permute-start = (f32[128,256]{1,0:T(8,128)S(1)}, f32[128,256]{1,0:T(8,128)S(1)}, u32[]{:S(2)}, u32[]{:S(2)}) collective-permute-start(f32[128,256]{1,0:T(8,128)S(1)} %total.1), channel_id=1, source_target_pairs={{0,16},{16,0},{32,48},{48,32},{64,80},{80,64},{96,112},{112,96},{1... | collective-permute-start | bytes 393224 | tf_op jit(solution)/shard_map/ppermute | solution.py:226
  33.9 11.8 %collective-permute-start.3 = (f32[128,256]{1,0:T(8,128)S(1)}, f32[128,256]{1,0:T(8,128)S(1)}, u32[]{:S(2)}, u32[]{:S(2)}) collective-permute-start(f32[128,256]{1,0:T(8,128)S(1)} %add.11), channel_id=1, source_target_pairs={{0,96},{16,112},{1,97},{17,113},{2,98},{18,114},{3,99},{19,115},{4... | collective-permute-start | bytes 393224 | tf_op jit(solution)/shard_map/ppermute | solution.py:229
  39.8 5.9 %collective-permute-start.2 = (f32[128,256]{1,0:T(8,128)S(1)}, f32[128,256]{1,0:T(8,128)S(1)}, u32[]{:S(2)}, u32[]{:S(2)}) collective-permute-start(f32[128,256]{1,0:T(8,128)S(1)} %add.11), channel_id=1, source_target_pairs={{0,64},{16,80},{32,96},{48,112},{1,65},{17,81},{33,97},{49,113},{2... | collective-permute-start | bytes 393224 | tf_op jit(solution)/shard_map/ppermute | solution.py:229
  41.1 5.9 %collective-permute-start.1 = (f32[128,256]{1,0:T(8,128)S(1)}, f32[128,256]{1,0:T(8,128)S(1)}, u32[]{:S(2)}, u32[]{:S(2)}) collective-permute-start(f32[128,256]{1,0:T(8,128)S(1)} %add.11), channel_id=1, source_target_pairs={{0,32},{16,48},{32,64},{48,80},{64,96},{80,112},{1,33},{17,49},{33... | collective-permute-start | bytes 393224 | tf_op jit(solution)/shard_map/ppermute | solution.py:229

commit v3 on v2

v3 whole, which is shorter than its diff:
```python
import jax
import jax.numpy as jnp
from jax import lax
from jax.experimental import pallas as pl
from jax.experimental.pallas import tpu as pltpu
from jax.sharding import PartitionSpec as P

HEADS = 16
DK = 128
GROUP = 64
ROWS = 128
SOURCES = 16
GROUPS = SOURCES * ROWS // GROUP
EDGE = 32
UNROLL = 2
LEVELS = DK // EDGE
PACK = DK // EDGE

f32, bf16 = jnp.float32, jnp.bfloat16
epsilon = 1e-06


def lanes(shape):
    return lax.broadcasted_iota(jnp.int32, shape, len(shape) - 1)


CHUNKS = 4


def unit_rows(values):
    values_f = values.astype(f32)
    scale_back = lax.rsqrt(jnp.sum(values_f * values_f, axis=-1, keepdims=True) + epsilon)
    return (values_f * scale_back).astype(bf16)


def unit_kernel(q_hbm, k_hbm, v_hbm, out_hbm, taken, ready, in_sems, out_sems):
    rows = ROWS // CHUNKS
    heads = HEADS // CHUNKS
    reads, writes = [], []
    for i, operand in enumerate((q_hbm, k_hbm, v_hbm)):
        for part in range(CHUNKS):
            piece = pl.ds(part * rows, rows)
            reads.append(pltpu.make_async_copy(operand.at[piece], taken.at[i, piece], in_sems.at[i, part]))
            reads[-1].start()
    for i in range(3):
        for part in range(CHUNKS):
            reads[i * CHUNKS + part].wait()
        for part in range(CHUNKS):
            for h in range(part * heads, (part + 1) * heads):
                values = taken[i, :, h * DK : (h + 1) * DK]
                ready[h, i] = values if i == 2 else unit_rows(values)
            piece = pl.ds(part * heads, heads)
            writes.append(pltpu.make_async_copy(ready.at[piece, i], out_hbm.at[piece, i], out_sems.at[i, part]))
            writes[-1].start()
    for write in writes:
        write.wait()


def total_kernel(qkv_ref, out_ref):
    def add(source, total):
        k = qkv_ref[source, ROWS : 2 * ROWS, :]
        v = qkv_ref[source, 2 * ROWS :, :]
        return total + turned_dot(k, jnp.concatenate([k, v], axis=1))

    out_ref[...] = lax.fori_loop(0, SOURCES, add, jnp.zeros((DK, 2 * DK), f32), unroll=True)


def token_kernel(mixed_ref, out_ref):
    for h in range(HEADS):
        out_ref[:, h * DK : (h + 1) * DK] = mixed_ref[h]


def turned_dot(left, right):
    return lax.dot_general(left, right, (((0,), (0,)), ((), ())), preferred_element_type=f32)


def dot(left, right):
    return jnp.dot(left, right, preferred_element_type=f32)


def spread(x, quarter):
    return jnp.take_along_axis(x, quarter * EDGE + lanes(x.shape) % EDGE, axis=1)


def left_parts(x):
    lane = lanes(x.shape)
    rest = x - x.astype(bf16).astype(f32)
    low = rest - rest.astype(bf16).astype(f32)
    first = jnp.where(lane < 3 * EDGE, x, rest).astype(bf16)
    second = jnp.where(lane < EDGE, rest, low).astype(bf16)
    return jnp.concatenate([first, second[:, : 2 * EDGE]], axis=1)


def right_parts(x):
    high = x.astype(bf16)
    rest = x - high.astype(f32)
    middle = rest.astype(bf16)
    low = (rest - middle.astype(f32)).astype(bf16)
    return jnp.concatenate([high, middle, low, high, middle, high], axis=0)


def two_parts(x):
    high = x.astype(bf16)
    return high, (x - high.astype(f32)).astype(bf16)


def invert(rows):
    lane = lanes((8, DK)) % EDGE
    base = lanes((8, DK)) - lane

    def pick(x, j):
        return jnp.take_along_axis(x, base + j, axis=1)

    for j in range(0, EDGE, 2):
        first, second = rows[j], rows[j + 1]
        a, b, d = pick(first, j), pick(first, j + 1), pick(second, j + 1)
        scale = 1.0 / (a * d - b * b)
        a, b, d = a * scale, b * scale, d * scale
        at_first, at_second = lane == j, lane == j + 1
        pivot_first = jnp.where(at_first, d, jnp.where(at_second, -b, d * first - b * second))
        pivot_second = jnp.where(at_first, -b, jnp.where(at_second, a, a * second - b * first))
        for r in [*range(j + 2, EDGE), *range(j)]:
            x = rows[r]
            kept = jnp.where(at_first | at_second, 0.0, x)
            rows[r] = kept - pick(x, j) * pivot_first - pick(x, j + 1) * pivot_second
        rows[j], rows[j + 1] = pivot_first, pivot_second
    return rows


def local_kernel(qkv_ref, gram_ref, vk_ref):
    gram_ref[0] = jnp.zeros((DK, DK), f32)
    vk_ref[0] = jnp.zeros((DK, DK), f32)
    per_source = ROWS // GROUP

    def add(c):
        source = c // per_source
        first = (c % per_source) * GROUP
        k = qkv_ref[source, ROWS + first : ROWS + first + GROUP, :]
        v = qkv_ref[source, 2 * ROWS + first : 2 * ROWS + first + GROUP, :]
        group = turned_dot(k, jnp.concatenate([k, v], axis=1))
        gram_ref[c + 1] = gram_ref[c] + group[:, :DK]
        vk_ref[c + 1] = vk_ref[c] + group[:, DK:]

    for c in range(GROUPS - 1):
        add(c)


def solve_kernel(
    seq_ref, qkv_ref, gram_ref, vk_ref, one_ref, two_ref, three_ref, partner_ref, ridge_ref, out_ref, work_even, work_odd, gram_start, vk_start, packed, panels
):
    row = lax.broadcasted_iota(jnp.int32, (DK, DK), 0)
    diagonal = jnp.where(row == lanes((DK, DK)), jnp.broadcast_to(ridge_ref[...], (DK, DK)), 0.0)
    seq = seq_ref[0]
    start = jnp.where(seq % 2 == 1, partner_ref[...], 0.0)
    for step, ref in enumerate((one_ref, two_ref, three_ref), 1):
        start = start + jnp.where(seq // 2 >= step, ref[...], 0.0)
    gram_start[...] = start[:, :DK] + diagonal
    vk_start[...] = start[:, DK:]

    per_source = ROWS // GROUP
    work = (work_even, work_odd)
    for level in range(LEVELS):
        before, after = work[level % 2], work[1 - level % 2]
        at = level * EDGE
        first = at + EDGE

        def pivot_rows(c):
            if level == 0:
                return gram_ref[c, at:first, :] + gram_start[at:first, :]
            return before[c, at:first, :]

        def rows_below(s, part):
            c = s * PACK + part
            if level > 0:
                return before[c, first:, :]
            source = s * (PACK // per_source) + part // per_source
            token = (part % per_source) * GROUP
            q = qkv_ref[source, token : token + GROUP, :].astype(f32)
            return jnp.concatenate([gram_ref[c, first:, :] + gram_start[first:, :], q], axis=0)

        for s in range(GROUPS // PACK):
            tile = None
            for part in range(PACK):
                block = pivot_rows(s * PACK + part)
                if part != level:
                    block = pltpu.roll(block, (EDGE * (part - level)) % DK, 1)
                tile = block if part == 0 else jnp.where(lanes(block.shape) // EDGE == part, block, tile)
            packed[pl.ds(s, EDGE, stride=8), :] = tile
        rows = invert([packed[8 * r : 8 * r + 8, :] for r in range(EDGE)])
        for r in range(EDGE):
            packed[8 * r : 8 * r + 8, :] = rows[r]

        def scale(s, _):
            tile = packed[pl.ds(s, EDGE, stride=8), :]
            for part in range(PACK):
                c = s * PACK + part
                inverse = spread(tile, part)
                panel = dot(left_parts(inverse), right_parts(pivot_rows(c)))
                panels[c] = right_parts(jnp.where(lanes(panel.shape) // EDGE == level, -inverse, panel))
            return 0

        def eliminate(s, _):
            for part in range(PACK):
                c = s * PACK + part
                below = rows_below(s, part)
                change = dot(left_parts(spread(below, level)), panels[c])
                after[c, first:, :] = jnp.where(lanes(below.shape) // EDGE == level, 0.0, below) - change
            return 0

        lax.fori_loop(0, GROUPS // PACK, scale, 0, unroll=UNROLL)
        lax.fori_loop(0, GROUPS // PACK, eliminate, 0, unroll=UNROLL)

    def apply(source, _):
        for half in range(per_source):
            c = source * per_source + half
            first = half * GROUP
            k = qkv_ref[source, ROWS + first : ROWS + first + GROUP, :]
            v = qkv_ref[source, 2 * ROWS + first : 2 * ROWS + first + GROUP, :]
            high, low = two_parts(work_even[c, DK:, :])
            vk_high, vk_low = two_parts(vk_ref[c] + vk_start[...])
            kk = jnp.concatenate([k, k], axis=1)
            scores = lax.dot_general(
                jnp.concatenate([high, low], axis=1),
                jnp.concatenate([kk, kk], axis=0),
                (((1,), (1,)), ((), ())),
                preferred_element_type=f32,
            )
            lane = lanes((GROUP, 2 * GROUP))
            causal = lane % GROUP <= lax.broadcasted_iota(jnp.int32, (GROUP, 2 * GROUP), 0)
            scores = jnp.where(causal, scores, 0.0)
            rest = scores - scores.astype(bf16).astype(f32)
            scores = jnp.where(lane < GROUP, scores, rest).astype(bf16)
            mixed = dot(
                jnp.concatenate([high, high, low, scores], axis=1),
                jnp.concatenate([vk_high, vk_low, vk_high, v, v], axis=0),
            )
            out_ref[source, first : first + GROUP, :] = mixed.astype(bf16)
        return 0

    lax.fori_loop(0, SOURCES, apply, 0, unroll=2)


def whole():
    return pl.BlockSpec(memory_space=pltpu.VMEM)


def body(queries, key_rows, value_rows, ridge_diag):
    seq = lax.axis_size("seq")
    qkv = pl.pallas_call(
        unit_kernel,
        out_shape=jax.ShapeDtypeStruct((HEADS, 3, ROWS, DK), bf16),
        in_specs=[pl.BlockSpec(memory_space=pl.ANY)] * 3,
        out_specs=pl.BlockSpec(memory_space=pl.ANY),
        scratch_shapes=[
            pltpu.VMEM((3, ROWS, HEADS * DK), bf16),
            pltpu.VMEM((HEADS, 3, ROWS, DK), bf16),
            pltpu.SemaphoreType.DMA((3, CHUNKS)),
            pltpu.SemaphoreType.DMA((3, CHUNKS)),
        ],
        name="unit",
    )(queries, key_rows, value_rows)
    qkv = qkv.reshape(HEADS, 3 * ROWS, DK)
    qkv = lax.all_to_all(qkv, "head", split_axis=0, concat_axis=0, tiled=True)
    total = pl.pallas_call(
        total_kernel,
        out_shape=jax.ShapeDtypeStruct((DK, 2 * DK), f32),
        in_specs=[whole()],
        out_specs=whole(),
        compiler_params=pltpu.CompilerParams(vmem_limit_bytes=6 * 2**20),
        name="total",
    )(qkv)
    partner = lax.ppermute(total, "seq", [(i, i ^ 1) for i in range(seq)])
    chip = total + partner
    earlier = [
        lax.ppermute(chip, "seq", [(i, (i + step) % seq) for i in range(seq)]) for step in range(2, seq, 2)
    ]
    grams, vks = pl.pallas_call(
        local_kernel,
        out_shape=[jax.ShapeDtypeStruct((GROUPS, DK, DK), f32)] * 2,
        in_specs=[whole()],
        out_specs=[whole()] * 2,
        cost_estimate=pl.CostEstimate(flops=2 * 2048 * 128 * 256, bytes_accessed=5 * 2**20, transcendentals=0),
        compiler_params=pltpu.CompilerParams(vmem_limit_bytes=8 * 2**20),
        name="local",
    )(qkv)
    ridge_here = lax.dynamic_slice_in_dim(ridge_diag, lax.axis_index("head"), 1, 0)
    where = lax.axis_index("seq").astype(jnp.int32).reshape(1)
    mixed = pl.pallas_call(
        solve_kernel,
        out_shape=jax.ShapeDtypeStruct((SOURCES, ROWS, DK), bf16),
        in_specs=[pl.BlockSpec(memory_space=pltpu.SMEM)] + [whole()] * 8,
        out_specs=whole(),
        scratch_shapes=[
            pltpu.VMEM((GROUPS, DK + GROUP, DK), f32),
            pltpu.VMEM((GROUPS, DK + GROUP, DK), f32),
            pltpu.VMEM((DK, DK), f32),
            pltpu.VMEM((DK, DK), f32),
            pltpu.VMEM((EDGE * 8, DK), f32),
            pltpu.VMEM((GROUPS, 6 * EDGE, DK), bf16),
        ],
        compiler_params=pltpu.CompilerParams(vmem_limit_bytes=16 * 2**20),
        name="solve",
    )(where, qkv, grams, vks, *earlier, partner, ridge_here)
    mixed = lax.all_to_all(mixed, "head", split_axis=0, concat_axis=0, tiled=True)
    return pl.pallas_call(
        token_kernel,
        out_shape=jax.ShapeDtypeStruct((ROWS, HEADS * DK), bf16),
        in_specs=[whole()],
        out_specs=whole(),
        compiler_params=pltpu.CompilerParams(vmem_limit_bytes=6 * 2**20),
        name="to_tokens",
    )(mixed)


def solution(mesh):
    in_specs = (P(("seq", "head"), None), P(("seq", "head"), None), P(("seq", "head"), None), P())
    out_specs = P(("seq", "head"), None)
    return jax.shard_map(body, mesh=mesh, in_specs=in_specs, out_specs=out_specs, check_vma=False)
```

time: 93.3 us -> 84.1 us (0.901); the launches traced: 92.1 us -> 83.9 us
  blocking collectives: 18 us -> 44.3 us
  starting transfers between devices: 20.9 us -> 5.45 us
  waiting for transfers between devices: 20.8 us -> 8.62 us
  Pallas kernels: 30.1 us -> 25.5 us
  local copies, waits for them, and re-layouts: 2.11 us -> 0.01 us
    all_to_all x0 -> x1, blocking collectives: none -> 29.9 us  [body(): qkv = lax.all_to_all(qkv, 'head', split_axis=0, concat_axis=0, tiled=True)]
    all_to_all x2 -> x0, waiting for transfers between devices: 16.5 us -> none  [the longest x1 16.5 us: body(): kv = lax.all_to_all(kv, 'head', split_axis=0, concat_axis=0, tiled=True)]
    all_to_all x2 -> x0, starting transfers between devices: 10.8 us -> none  [the longest x1 7.25 us: body(): kv = lax.all_to_all(kv, 'head', split_axis=0, concat_axis=0, tiled=True)]
    pallas_call x1, Pallas kernels: 26.2 us -> 20.5 us  [body(): pl.pallas_call(solve_kernel, out_shape=jax.ShapeDtypeStruct((SOURCES, ROW...]
    ppermute x3, starting transfers between devices: 10 us -> 5.36 us  [body(): lax.ppermute(chip, 'seq', [(i, (i + step) % seq) for i in range(seq)])]
    ppermute x3, waiting for transfers between devices: 3.03 us -> 7.28 us  [body(): lax.ppermute(chip, 'seq', [(i, (i + step) % seq) for i in range(seq)])]
    all_to_all x1, blocking collectives: 18 us -> 14.4 us  [body(): lax.all_to_all(mixed, 'head', split_axis=0, concat_axis=0, tiled=True)]
    unnamed x8 -> x2, local copies, waits for them, and re-layouts: 2.1 us -> 0.01 us
  transfers between devices with their start and end apart: 6 -> 4, of which waited for: 4 -> 4; matrix products, arithmetic and copies ran while one was open for 0% -> 0% of each run, Pallas kernels for 2% -> 1%
where the time goes in v3:
time: 84.1 us; the launch traced here: 83.9 us
  blocking collectives  44.3 us (53%)
  Pallas kernels  25.5 us (30%)
  waiting for transfers between devices  8.62 us (10%)
  starting transfers between devices  5.45 us (6%)
    all_to_all x1, blocking collectives, body(): qkv = lax.all_to_all(qkv, 'head', split_axis=0, concat_axis=0, tiled=True)  29.9 us
    pallas_call x1, Pallas kernels, body(): pl.pallas_call(solve_kernel, out_shape=jax.ShapeDtypeStruct((SOURCES, ROW...  20.5 us
    all_to_all x1, blocking collectives, body(): lax.all_to_all(mixed, 'head', split_axis=0, concat_axis=0, tiled=True)  14.4 us
    ppermute x3, waiting for transfers between devices, body(): lax.ppermute(chip, 'seq', [(i, (i + step) % seq) for i in range(seq)])  7.28 us
    ppermute x3, starting transfers between devices, body(): lax.ppermute(chip, 'seq', [(i, (i + step) % seq) for i in range(seq)])  5.36 us
    pallas_call x1, Pallas kernels, body(): pl.pallas_call(unit_kernel, out_shape=jax.ShapeDtypeStruct((HEADS, 3, ROW...  2.88 us
  transfers between devices with their start and end apart: 4, of which 4 were waited for; matrix products, arithmetic and copies ran while one was open for 0% of the time, Pallas kernels for 1%

profile of v3, /device:TPU:0, one launch (start us, length us, event | category | flops | bytes accessed | tf_op | source)
XLA Modules:
  0.0 83.9 jit_solution(17298000987405885732)
XLA Ops:
  0.0 0.0 copy-start
  0.0 2.9 %unit.1 = bf16[16,3,128,128]{3,2,1,0:T(8,128)(2,1)} custom-call(bf16[128,2048]{1,0:T(8,128)(2,1)} %q_hbm.1, bf16[128,2048]{1,0:T(8,128)(2,1)} %k_hbm.1, bf16[128,2048]{1,0:T(8,128)(2,1)} %v_hbm.1), custom_call_target="tpu_custom_call" | custom-call | tf_op jit(solution)/shard_map/unit/pallas_call | solution.py:249
  2.9 29.9 %all_to_all.10.qkv_ref = bf16[16,384,128]{2,1,0:T(8,128)(2,1)S(1)} all-to-all(bf16[16,384,128]{2,1,0:T(8,128)(2,1)} %bitcast.2), channel_id=1, replica_groups=mesh['seq'=8,'head'=16] {'head'}, dimensions={0} | all-to-all | bytes 3145728 | tf_op jit(solution)/shard_map/all_to_all | solution.py:263
  32.8 0.5 total.1
  33.3 0.1 collective-permute-start
  33.4 1.3 %collective-permute-done.partner_ref = f32[128,256]{1,0:T(8,128)S(1)} collective-permute-done((f32[128,256]{1,0:T(8,128)S(1)}, f32[128,256]{1,0:T(8,128)S(1)}, u32[]{:S(2)}, u32[]{:S(2)}) %collective-permute-start) | collective-permute-done | bytes 131104 | tf_op jit(solution)/shard_map/ppermute | solution.py:272
  34.7 4.1 %collective-permute-start.3 = (f32[128,256]{1,0:T(8,128)S(1)}, f32[128,256]{1,0:T(8,128)S(1)}, u32[]{:S(2)}, u32[]{:S(2)}) collective-permute-start(f32[128,256]{1,0:T(8,128)S(1)} %add.6), channel_id=1, source_target_pairs={{0,96},{16,112},{32,0},{48,16},{64,32},{80,48},{96,64},{112,80},{1... | collective-permute-start | bytes 393224 | tf_op jit(solution)/shard_map/ppermute | solution.py:275
  38.8 0.0 collective-permute-start.2
  38.8 1.3 %collective-permute-start.1 = (f32[128,256]{1,0:T(8,128)S(1)}, f32[128,256]{1,0:T(8,128)S(1)}, u32[]{:S(2)}, u32[]{:S(2)}) collective-permute-start(f32[128,256]{1,0:T(8,128)S(1)} %add.6), channel_id=1, source_target_pairs={{0,32},{16,48},{32,64},{48,80},{64,96},{80,112},{96,0},{112,16},{1... | collective-permute-start | bytes 393224 | tf_op jit(solution)/shard_map/ppermute | solution.py:275
  40.1 0.0 copy-done
  40.1 0.7 local.1
  40.8 3.9 %collective-permute-done.3.three_ref = f32[128,256]{1,0:T(8,128)S(1)} collective-permute-done((f32[128,256]{1,0:T(8,128)S(1)}, f32[128,256]{1,0:T(8,128)S(1)}, u32[]{:S(2)}, u32[]{:S(2)}) %collective-permute-start.3) | collective-permute-done | bytes 131104 | tf_op jit(solution)/shard_map/ppermute | solution.py:275
  44.7 2.0 %collective-permute-done.2.two_ref = f32[128,256]{1,0:T(8,128)S(1)} collective-permute-done((f32[128,256]{1,0:T(8,128)S(1)}, f32[128,256]{1,0:T(8,128)S(1)}, u32[]{:S(2)}, u32[]{:S(2)}) %collective-permute-start.2) | collective-permute-done | bytes 131104 | tf_op jit(solution)/shard_map/ppermute | solution.py:275
  46.7 1.4 %collective-permute-done.1.one_ref = f32[128,256]{1,0:T(8,128)S(1)} collective-permute-done((f32[128,256]{1,0:T(8,128)S(1)}, f32[128,256]{1,0:T(8,128)S(1)}, u32[]{:S(2)}, u32[]{:S(2)}) %collective-permute-start.1) | collective-permute-done | bytes 131104 | tf_op jit(solution)/shard_map/ppermute | solution.py:275
  48.1 20.5 %solve.1 = bf16[16,128,128]{2,1,0:T(8,128)(2,1)S(1)} custom-call(s32[1]{0:T(128)} %bitcast.seq_ref, bf16[16,384,128]{2,1,0:T(8,128)(2,1)S(1)} %all_to_all.10.qkv_ref, f32[32,128,128]{2,1,0:T(8,128)S(1)} %get-tuple-element.7.gram_ref, f32[32,128,128]{2,1,0:T(8,128)S(1)} %get-tuple-element.8.vk_ref, f32[128,256]{1,0:T(8,128)S(1)} %collective-permute-done.1.one_ref, ...), custom_call_target="tpu_custom_call" | custom-call | tf_op jit(solution)/shard_map/solve/pallas_call | solution.py:288
  68.6 14.4 %all_to_all.11.mixed_ref = bf16[16,128,128]{2,1,0:T(8,128)(2,1)S(1)} all-to-all(bf16[16,128,128]{2,1,0:T(8,128)(2,1)S(1)} %solve.1), channel_id=1, replica_groups=mesh['seq'=8,'head'=16] {'head'}, dimensions={0} | all-to-all | bytes 1048576 | tf_op jit(solution)/shard_map/all_to_all | solution.py:304
  83.0 0.9 %to_tokens.1 = bf16[128,2048]{1,0:T(8,128)(2,1)} custom-call(bf16[16,128,128]{2,1,0:T(8,128)(2,1)S(1)} %all_to_all.11.mixed_ref), custom_call_target="tpu_custom_call" | custom-call | tf_op jit(solution)/shard_map/to_tokens/pallas_call | solution.py:305
  (2 shorter events, 0.0 us)
Async XLA Ops:
  0.0 40.1 %copy-start = (f32[16,128]{1,0:T(8,128)S(1)}, f32[16,128]{1,0:T(8,128)}, u32[]{:S(2)}) copy-start(f32[16,128]{1,0:T(8,128)} %param.7) | copy-start | bytes 24580
  33.3 1.4 %collective-permute-start = (f32[128,256]{1,0:T(8,128)S(1)}, f32[128,256]{1,0:T(8,128)S(1)}, u32[]{:S(2)}, u32[]{:S(2)}) collective-permute-start(f32[128,256]{1,0:T(8,128)S(1)} %total.1), channel_id=1, source_target_pairs={{0,16},{16,0},{32,48},{48,32},{64,80},{80,64},{96,112},{112,96},{1... | collective-permute-start | bytes 393224 | tf_op jit(solution)/shard_map/ppermute | solution.py:272
  34.7 10.0 %collective-permute-start.3 = (f32[128,256]{1,0:T(8,128)S(1)}, f32[128,256]{1,0:T(8,128)S(1)}, u32[]{:S(2)}, u32[]{:S(2)}) collective-permute-start(f32[128,256]{1,0:T(8,128)S(1)} %add.6), channel_id=1, source_target_pairs={{0,96},{16,112},{32,0},{48,16},{64,32},{80,48},{96,64},{112,80},{1... | collective-permute-start | bytes 393224 | tf_op jit(solution)/shard_map/ppermute | solution.py:275
  38.8 7.9 %collective-permute-start.2 = (f32[128,256]{1,0:T(8,128)S(1)}, f32[128,256]{1,0:T(8,128)S(1)}, u32[]{:S(2)}, u32[]{:S(2)}) collective-permute-start(f32[128,256]{1,0:T(8,128)S(1)} %add.6), channel_id=1, source_target_pairs={{0,64},{16,80},{32,96},{48,112},{64,0},{80,16},{96,32},{112,48},{1... | collective-permute-start | bytes 393224 | tf_op jit(solution)/shard_map/ppermute | solution.py:275
  38.8 9.3 %collective-permute-start.1 = (f32[128,256]{1,0:T(8,128)S(1)}, f32[128,256]{1,0:T(8,128)S(1)}, u32[]{:S(2)}, u32[]{:S(2)}) collective-permute-start(f32[128,256]{1,0:T(8,128)S(1)} %add.6), channel_id=1, source_target_pairs={{0,32},{16,48},{32,64},{48,80},{64,96},{80,112},{96,0},{112,16},{1... | collective-permute-start | bytes 393224 | tf_op jit(solution)/shard_map/ppermute | solution.py:275

commit v4 on v3

--- a/solution.py
+++ b/solution.py
@@ -12,7 +12,6 @@
 SOURCES = 16
 GROUPS = SOURCES * ROWS // GROUP
 EDGE = 32
-UNROLL = 2
 LEVELS = DK // EDGE
 PACK = DK // EDGE
 
@@ -65,9 +64,14 @@
     out_ref[...] = lax.fori_loop(0, SOURCES, add, jnp.zeros((DK, 2 * DK), f32), unroll=True)
 
 
-def token_kernel(mixed_ref, out_ref):
-    for h in range(HEADS):
-        out_ref[:, h * DK : (h + 1) * DK] = mixed_ref[h]
+def token_kernel(mixed_hbm, out_hbm, sems):
+    copies = [
+        pltpu.make_async_copy(mixed_hbm.at[h], out_hbm.at[:, pl.ds(h * DK, DK)], sems.at[h]) for h in range(HEADS)
+    ]
+    for copy in copies:
+        copy.start()
+    for copy in copies:
+        copy.wait()
 
 
 def turned_dot(left, right):
@@ -207,8 +211,8 @@
                 after[c, first:, :] = jnp.where(lanes(below.shape) // EDGE == level, 0.0, below) - change
             return 0
 
-        lax.fori_loop(0, GROUPS // PACK, scale, 0, unroll=UNROLL)
-        lax.fori_loop(0, GROUPS // PACK, eliminate, 0, unroll=UNROLL)
+        lax.fori_loop(0, GROUPS // PACK, scale, 0, unroll=True)
+        lax.fori_loop(0, GROUPS // PACK, eliminate, 0, unroll=True)
 
     def apply(source, _):
         for half in range(per_source):
@@ -237,7 +241,7 @@
             out_ref[source, first : first + GROUP, :] = mixed.astype(bf16)
         return 0
 
-    lax.fori_loop(0, SOURCES, apply, 0, unroll=2)
+    lax.fori_loop(0, SOURCES, apply, 0, unroll=True)
 
 
 def whole():
@@ -305,9 +309,10 @@
     return pl.pallas_call(
         token_kernel,
         out_shape=jax.ShapeDtypeStruct((ROWS, HEADS * DK), bf16),
-        in_specs=[whole()],
-        out_specs=whole(),
-        compiler_params=pltpu.CompilerParams(vmem_limit_bytes=6 * 2**20),
+        in_specs=[pl.BlockSpec(memory_space=pl.ANY)],
+        out_specs=pl.BlockSpec(memory_space=pl.ANY),
+        scratch_shapes=[pltpu.SemaphoreType.DMA((HEADS,))],
+        compiler_params=pltpu.CompilerParams(vmem_limit_bytes=4 * 2**20),
         name="to_tokens",
     )(mixed)
 

time: 84.1 us -> 77.9 us (0.926)
  Pallas kernels: 25.5 us -> 19.1 us
    pallas_call x1, Pallas kernels: 20.5 us -> 14.2 us  [body(): pl.pallas_call(solve_kernel, out_shape=jax.ShapeDtypeStruct((SOURCES, ROW...]
where the time goes in v4:
time: 77.9 us; the launch traced here: 77.7 us
  blocking collectives  44.3 us (57%)
  Pallas kernels  19.1 us (25%)
  waiting for transfers between devices  8.61 us (11%)
  starting transfers between devices  5.45 us (7%)
    all_to_all x1, blocking collectives, body(): qkv = lax.all_to_all(qkv, 'head', split_axis=0, concat_axis=0, tiled=True)  29.9 us
    all_to_all x1, blocking collectives, body(): lax.all_to_all(mixed, 'head', split_axis=0, concat_axis=0, tiled=True)  14.4 us
    pallas_call x1, Pallas kernels, body(): pl.pallas_call(solve_kernel, out_shape=jax.ShapeDtypeStruct((SOURCES, ROW...  14.2 us
    ppermute x3, waiting for transfers between devices, body(): lax.ppermute(chip, 'seq', [(i, (i + step) % seq) for i in range(seq)])  7.28 us
    ppermute x3, starting transfers between devices, body(): lax.ppermute(chip, 'seq', [(i, (i + step) % seq) for i in range(seq)])  5.37 us
    pallas_call x1, Pallas kernels, body(): pl.pallas_call(unit_kernel, out_shape=jax.ShapeDtypeStruct((HEADS, 3, ROW...  2.88 us
  transfers between devices with their start and end apart: 4, of which 4 were waited for; matrix products, arithmetic and copies ran while one was open for 0% of the time, Pallas kernels for 1%

profile of v4, /device:TPU:0, one launch (start us, length us, event | category | flops | bytes accessed | tf_op | source)
XLA Modules:
  0.0 77.7 jit_solution(584323890309793239)
XLA Ops:
  0.0 0.0 copy-start
  0.0 2.9 %unit.1 = bf16[16,3,128,128]{3,2,1,0:T(8,128)(2,1)} custom-call(bf16[128,2048]{1,0:T(8,128)(2,1)} %q_hbm.1, bf16[128,2048]{1,0:T(8,128)(2,1)} %k_hbm.1, bf16[128,2048]{1,0:T(8,128)(2,1)} %v_hbm.1), custom_call_target="tpu_custom_call" | custom-call | tf_op jit(solution)/shard_map/unit/pallas_call | solution.py:253
  2.9 29.9 %all_to_all.10.qkv_ref = bf16[16,384,128]{2,1,0:T(8,128)(2,1)S(1)} all-to-all(bf16[16,384,128]{2,1,0:T(8,128)(2,1)} %bitcast.2), channel_id=1, replica_groups=mesh['seq'=8,'head'=16] {'head'}, dimensions={0} | all-to-all | bytes 3145728 | tf_op jit(solution)/shard_map/all_to_all | solution.py:267
  32.8 0.5 total.1
  33.3 0.1 collective-permute-start
  33.4 1.3 %collective-permute-done.partner_ref = f32[128,256]{1,0:T(8,128)S(1)} collective-permute-done((f32[128,256]{1,0:T(8,128)S(1)}, f32[128,256]{1,0:T(8,128)S(1)}, u32[]{:S(2)}, u32[]{:S(2)}) %collective-permute-start) | collective-permute-done | bytes 131104 | tf_op jit(solution)/shard_map/ppermute | solution.py:276
  34.7 4.1 %collective-permute-start.3 = (f32[128,256]{1,0:T(8,128)S(1)}, f32[128,256]{1,0:T(8,128)S(1)}, u32[]{:S(2)}, u32[]{:S(2)}) collective-permute-start(f32[128,256]{1,0:T(8,128)S(1)} %add.6), channel_id=1, source_target_pairs={{0,96},{16,112},{32,0},{48,16},{64,32},{80,48},{96,64},{112,80},{1... | collective-permute-start | bytes 393224 | tf_op jit(solution)/shard_map/ppermute | solution.py:279
  38.8 0.0 collective-permute-start.2
  38.8 1.3 %collective-permute-start.1 = (f32[128,256]{1,0:T(8,128)S(1)}, f32[128,256]{1,0:T(8,128)S(1)}, u32[]{:S(2)}, u32[]{:S(2)}) collective-permute-start(f32[128,256]{1,0:T(8,128)S(1)} %add.6), channel_id=1, source_target_pairs={{0,32},{16,48},{32,64},{48,80},{64,96},{80,112},{96,0},{112,16},{1... | collective-permute-start | bytes 393224 | tf_op jit(solution)/shard_map/ppermute | solution.py:279
  40.1 0.0 copy-done
  40.1 0.7 local.1
  40.8 3.9 %collective-permute-done.3.three_ref = f32[128,256]{1,0:T(8,128)S(1)} collective-permute-done((f32[128,256]{1,0:T(8,128)S(1)}, f32[128,256]{1,0:T(8,128)S(1)}, u32[]{:S(2)}, u32[]{:S(2)}) %collective-permute-start.3) | collective-permute-done | bytes 131104 | tf_op jit(solution)/shard_map/ppermute | solution.py:279
  44.7 2.0 %collective-permute-done.2.two_ref = f32[128,256]{1,0:T(8,128)S(1)} collective-permute-done((f32[128,256]{1,0:T(8,128)S(1)}, f32[128,256]{1,0:T(8,128)S(1)}, u32[]{:S(2)}, u32[]{:S(2)}) %collective-permute-start.2) | collective-permute-done | bytes 131104 | tf_op jit(solution)/shard_map/ppermute | solution.py:279
  46.7 1.4 %collective-permute-done.1.one_ref = f32[128,256]{1,0:T(8,128)S(1)} collective-permute-done((f32[128,256]{1,0:T(8,128)S(1)}, f32[128,256]{1,0:T(8,128)S(1)}, u32[]{:S(2)}, u32[]{:S(2)}) %collective-permute-start.1) | collective-permute-done | bytes 131104 | tf_op jit(solution)/shard_map/ppermute | solution.py:279
  48.1 14.2 %solve.1 = bf16[16,128,128]{2,1,0:T(8,128)(2,1)S(1)} custom-call(s32[1]{0:T(128)} %bitcast.seq_ref, bf16[16,384,128]{2,1,0:T(8,128)(2,1)S(1)} %all_to_all.10.qkv_ref, f32[32,128,128]{2,1,0:T(8,128)S(1)} %get-tuple-element.7.gram_ref, f32[32,128,128]{2,1,0:T(8,128)S(1)} %get-tuple-element.8.vk_ref, f32[128,256]{1,0:T(8,128)S(1)} %collective-permute-done.1.one_ref, ...), custom_call_target="tpu_custom_call" | custom-call | tf_op jit(solution)/shard_map/solve/pallas_call | solution.py:292
  62.3 14.4 %all_to_all.11.mixed_hbm = bf16[16,128,128]{2,1,0:T(8,128)(2,1)S(1)} all-to-all(bf16[16,128,128]{2,1,0:T(8,128)(2,1)S(1)} %solve.1), channel_id=1, replica_groups=mesh['seq'=8,'head'=16] {'head'}, dimensions={0} | all-to-all | bytes 1048576 | tf_op jit(solution)/shard_map/all_to_all | solution.py:308
  76.6 0.9 %to_tokens.1 = bf16[128,2048]{1,0:T(8,128)(2,1)} custom-call(bf16[16,128,128]{2,1,0:T(8,128)(2,1)S(1)} %all_to_all.11.mixed_hbm), custom_call_target="tpu_custom_call" | custom-call | tf_op jit(solution)/shard_map/to_tokens/pallas_call | solution.py:309
  (2 shorter events, 0.0 us)
Async XLA Ops:
  0.0 40.1 %copy-start = (f32[16,128]{1,0:T(8,128)S(1)}, f32[16,128]{1,0:T(8,128)}, u32[]{:S(2)}) copy-start(f32[16,128]{1,0:T(8,128)} %param.7) | copy-start | bytes 24580
  33.3 1.4 %collective-permute-start = (f32[128,256]{1,0:T(8,128)S(1)}, f32[128,256]{1,0:T(8,128)S(1)}, u32[]{:S(2)}, u32[]{:S(2)}) collective-permute-start(f32[128,256]{1,0:T(8,128)S(1)} %total.1), channel_id=1, source_target_pairs={{0,16},{16,0},{32,48},{48,32},{64,80},{80,64},{96,112},{112,96},{1... | collective-permute-start | bytes 393224 | tf_op jit(solution)/shard_map/ppermute | solution.py:276
  34.7 10.0 %collective-permute-start.3 = (f32[128,256]{1,0:T(8,128)S(1)}, f32[128,256]{1,0:T(8,128)S(1)}, u32[]{:S(2)}, u32[]{:S(2)}) collective-permute-start(f32[128,256]{1,0:T(8,128)S(1)} %add.6), channel_id=1, source_target_pairs={{0,96},{16,112},{32,0},{48,16},{64,32},{80,48},{96,64},{112,80},{1... | collective-permute-start | bytes 393224 | tf_op jit(solution)/shard_map/ppermute | solution.py:279
  38.8 7.9 %collective-permute-start.2 = (f32[128,256]{1,0:T(8,128)S(1)}, f32[128,256]{1,0:T(8,128)S(1)}, u32[]{:S(2)}, u32[]{:S(2)}) collective-permute-start(f32[128,256]{1,0:T(8,128)S(1)} %add.6), channel_id=1, source_target_pairs={{0,64},{16,80},{32,96},{48,112},{64,0},{80,16},{96,32},{112,48},{1... | collective-permute-start | bytes 393224 | tf_op jit(solution)/shard_map/ppermute | solution.py:279
  38.8 9.3 %collective-permute-start.1 = (f32[128,256]{1,0:T(8,128)S(1)}, f32[128,256]{1,0:T(8,128)S(1)}, u32[]{:S(2)}, u32[]{:S(2)}) collective-permute-start(f32[128,256]{1,0:T(8,128)S(1)} %add.6), channel_id=1, source_target_pairs={{0,32},{16,48},{32,64},{48,80},{64,96},{80,112},{96,0},{112,16},{1... | collective-permute-start | bytes 393224 | tf_op jit(solution)/shard_map/ppermute | solution.py:279

commit v5 on v4

--- a/solution.py
+++ b/solution.py
@@ -61,7 +61,9 @@
         v = qkv_ref[source, 2 * ROWS :, :]
         return total + turned_dot(k, jnp.concatenate([k, v], axis=1))
 
-    out_ref[...] = lax.fori_loop(0, SOURCES, add, jnp.zeros((DK, 2 * DK), f32), unroll=True)
+    total = lax.fori_loop(0, SOURCES, add, jnp.zeros((DK, 2 * DK), f32), unroll=True)
+    out_ref[:DK, :] = total[:, :DK]
+    out_ref[DK:, :] = total[:, DK:]
 
 
 def token_kernel(mixed_hbm, out_hbm, sems):
@@ -149,17 +151,20 @@
         add(c)
 
 
+def earlier_sum(seq, partner, steps):
+    start = jnp.where(seq % 2 == 1, partner, 0.0)
+    for step, ref in enumerate(steps, 1):
+        start = start + jnp.where(seq // 2 >= step, ref[...], 0.0)
+    return start
+
+
 def solve_kernel(
-    seq_ref, qkv_ref, gram_ref, vk_ref, one_ref, two_ref, three_ref, partner_ref, ridge_ref, out_ref, work_even, work_odd, gram_start, vk_start, packed, panels
+    seq_ref, qkv_ref, gram_ref, one_ref, two_ref, three_ref, partner_ref, ridge_ref, solved_ref, work_even, work_odd, gram_start, packed, panels
 ):
     row = lax.broadcasted_iota(jnp.int32, (DK, DK), 0)
     diagonal = jnp.where(row == lanes((DK, DK)), jnp.broadcast_to(ridge_ref[...], (DK, DK)), 0.0)
-    seq = seq_ref[0]
-    start = jnp.where(seq % 2 == 1, partner_ref[...], 0.0)
-    for step, ref in enumerate((one_ref, two_ref, three_ref), 1):
-        start = start + jnp.where(seq // 2 >= step, ref[...], 0.0)
-    gram_start[...] = start[:, :DK] + diagonal
-    vk_start[...] = start[:, DK:]
+    start = earlier_sum(seq_ref[0], partner_ref[:DK, :], (one_ref, two_ref, three_ref))
+    gram_start[...] = start + diagonal
 
     per_source = ROWS // GROUP
     work = (work_even, work_odd)
@@ -208,11 +213,20 @@
                 c = s * PACK + part
                 below = rows_below(s, part)
                 change = dot(left_parts(spread(below, level)), panels[c])
-                after[c, first:, :] = jnp.where(lanes(below.shape) // EDGE == level, 0.0, below) - change
+                below = jnp.where(lanes(below.shape) // EDGE == level, 0.0, below) - change
+                if level < LEVELS - 1:
+                    after[c, first:, :] = below
+                else:
+                    solved_ref[c] = below
             return 0
 
         lax.fori_loop(0, GROUPS // PACK, scale, 0, unroll=True)
         lax.fori_loop(0, GROUPS // PACK, eliminate, 0, unroll=True)
+
+
+def mix_kernel(seq_ref, solved_ref, qkv_ref, vk_ref, one_ref, two_ref, three_ref, partner_ref, out_ref, vk_start):
+    vk_start[...] = earlier_sum(seq_ref[0], partner_ref[DK:, :], (one_ref, two_ref, three_ref))
+    per_source = ROWS // GROUP
 
     def apply(source, _):
         for half in range(per_source):
@@ -220,7 +234,7 @@
             first = half * GROUP
             k = qkv_ref[source, ROWS + first : ROWS + first + GROUP, :]
             v = qkv_ref[source, 2 * ROWS + first : 2 * ROWS + first + GROUP, :]
-            high, low = two_parts(work_even[c, DK:, :])
+            high, low = two_parts(solved_ref[c])
             vk_high, vk_low = two_parts(vk_ref[c] + vk_start[...])
             kk = jnp.concatenate([k, k], axis=1)
             scores = lax.dot_general(
@@ -267,17 +281,20 @@
     qkv = lax.all_to_all(qkv, "head", split_axis=0, concat_axis=0, tiled=True)
     total = pl.pallas_call(
         total_kernel,
-        out_shape=jax.ShapeDtypeStruct((DK, 2 * DK), f32),
+        out_shape=jax.ShapeDtypeStruct((2 * DK, DK), f32),
         in_specs=[whole()],
         out_specs=whole(),
         compiler_params=pltpu.CompilerParams(vmem_limit_bytes=6 * 2**20),
         name="total",
     )(qkv)
     partner = lax.ppermute(total, "seq", [(i, i ^ 1) for i in range(seq)])
-    chip = total + partner
-    earlier = [
-        lax.ppermute(chip, "seq", [(i, (i + step) % seq) for i in range(seq)]) for step in range(2, seq, 2)
-    ]
+    def from_earlier(chip):
+        return [
+            lax.ppermute(chip, "seq", [(i, (i + step) % seq) for i in range(seq)]) for step in range(2, seq, 2)
+        ]
+
+    gram_steps = from_earlier(total[:DK] + partner[:DK])
+    vk_steps = from_earlier(total[DK:] + partner[DK:])
     grams, vks = pl.pallas_call(
         local_kernel,
         out_shape=[jax.ShapeDtypeStruct((GROUPS, DK, DK), f32)] * 2,
@@ -289,22 +306,32 @@
     )(qkv)
     ridge_here = lax.dynamic_slice_in_dim(ridge_diag, lax.axis_index("head"), 1, 0)
     where = lax.axis_index("seq").astype(jnp.int32).reshape(1)
-    mixed = pl.pallas_call(
+    scalar = pl.BlockSpec(memory_space=pltpu.SMEM)
+    solved = pl.pallas_call(
         solve_kernel,
-        out_shape=jax.ShapeDtypeStruct((SOURCES, ROWS, DK), bf16),
-        in_specs=[pl.BlockSpec(memory_space=pltpu.SMEM)] + [whole()] * 8,
+        out_shape=jax.ShapeDtypeStruct((GROUPS, GROUP, DK), f32),
+        in_specs=[scalar] + [whole()] * 7,
         out_specs=whole(),
         scratch_shapes=[
             pltpu.VMEM((GROUPS, DK + GROUP, DK), f32),
             pltpu.VMEM((GROUPS, DK + GROUP, DK), f32),
             pltpu.VMEM((DK, DK), f32),
-            pltpu.VMEM((DK, DK), f32),
             pltpu.VMEM((EDGE * 8, DK), f32),
             pltpu.VMEM((GROUPS, 6 * EDGE, DK), bf16),
         ],
+        cost_estimate=pl.CostEstimate(flops=10**10, bytes_accessed=30 * 2**20, transcendentals=0),
         compiler_params=pltpu.CompilerParams(vmem_limit_bytes=16 * 2**20),
         name="solve",
-    )(where, qkv, grams, vks, *earlier, partner, ridge_here)
+    )(where, qkv, grams, *gram_steps, partner, ridge_here)
+    mixed = pl.pallas_call(
+        mix_kernel,
+        out_shape=jax.ShapeDtypeStruct((SOURCES, ROWS, DK), bf16),
+        in_specs=[scalar] + [whole()] * 7,
+        out_specs=whole(),
+        scratch_shapes=[pltpu.VMEM((DK, DK), f32)],
+        compiler_params=pltpu.CompilerParams(vmem_limit_bytes=8 * 2**20),
+        name="mix",
+    )(where, solved, qkv, vks, *vk_steps, partner)
     mixed = lax.all_to_all(mixed, "head", split_axis=0, concat_axis=0, tiled=True)
     return pl.pallas_call(
         token_kernel,

time: 77.9 us -> 74.4 us (0.955)
  waiting for transfers between devices: 8.61 us -> 1.35 us
  starting transfers between devices: 5.45 us -> 10.5 us
  blocking collectives: 44.3 us -> 43.3 us
    ppermute x3 -> x6, waiting for transfers between devices: 7.28 us -> 0.02 us  [from_earlier(): lax.ppermute(chip, 'seq', [(i, (i + step) % seq) for i in range(seq)])]
    ppermute x3 -> x6, starting transfers between devices: 5.37 us -> 10.4 us  [from_earlier(): lax.ppermute(chip, 'seq', [(i, (i + step) % seq) for i in range(seq)])]
    all_to_all x1, blocking collectives: 14.4 us -> 13.4 us  [body(): lax.all_to_all(mixed, 'head', split_axis=0, concat_axis=0, tiled=True)]
    pallas_call x2 -> x3, Pallas kernels: 14.6 us -> 14.2 us  [the longest x1 12.2 us: body(): pl.pallas_call(solve_kernel, out_shape=jax.ShapeDtypeStruct((GROUPS, GROU...]
  transfers between devices with their start and end apart: 4 -> 7, of which waited for: 4 -> 1; matrix products, arithmetic and copies ran while one was open for 0% -> 0% of each run, Pallas kernels for 1% -> 17%
where the time goes in v5:
time: 74.4 us; the launch traced here: 74.2 us
  blocking collectives  43.3 us (58%)
  Pallas kernels  18.7 us (25%)
  starting transfers between devices  10.5 us (14%)
  waiting for transfers between devices  1.35 us (2%)
    all_to_all x1, blocking collectives, body(): qkv = lax.all_to_all(qkv, 'head', split_axis=0, concat_axis=0, tiled=True)  29.9 us
    all_to_all x1, blocking collectives, body(): lax.all_to_all(mixed, 'head', split_axis=0, concat_axis=0, tiled=True)  13.4 us
    pallas_call x1, Pallas kernels, body(): pl.pallas_call(solve_kernel, out_shape=jax.ShapeDtypeStruct((GROUPS, GROU...  12.2 us
    ppermute x6, starting transfers between devices, from_earlier(): lax.ppermute(chip, 'seq', [(i, (i + step) % seq) for i in range(seq)])  10.4 us
    pallas_call x1, Pallas kernels, body(): pl.pallas_call(unit_kernel, out_shape=jax.ShapeDtypeStruct((HEADS, 3, ROW...  2.88 us
    pallas_call x1, Pallas kernels, body(): pl.pallas_call(mix_kernel, out_shape=jax.ShapeDtypeStruct((SOURCES, ROWS,...  1.54 us
  transfers between devices with their start and end apart: 7, of which 1 were waited for; matrix products, arithmetic and copies ran while one was open for 0% of the time, Pallas kernels for 17%

profile of v5, /device:TPU:0, one launch (start us, length us, event | category | flops | bytes accessed | tf_op | source)
XLA Modules:
  0.0 74.2 jit_solution(7076327282923431648)
XLA Ops:
  0.0 0.0 copy-start
  0.0 2.9 %unit.1 = bf16[16,3,128,128]{3,2,1,0:T(8,128)(2,1)} custom-call(bf16[128,2048]{1,0:T(8,128)(2,1)} %q_hbm.1, bf16[128,2048]{1,0:T(8,128)(2,1)} %k_hbm.1, bf16[128,2048]{1,0:T(8,128)(2,1)} %v_hbm.1), custom_call_target="tpu_custom_call" | custom-call | tf_op jit(solution)/shard_map/unit/pallas_call | solution.py:267
  2.9 29.9 %all_to_all.10.qkv_ref = bf16[16,384,128]{2,1,0:T(8,128)(2,1)S(1)} all-to-all(bf16[16,384,128]{2,1,0:T(8,128)(2,1)} %bitcast.2), channel_id=1, replica_groups=mesh['seq'=8,'head'=16] {'head'}, dimensions={0} | all-to-all | bytes 3145728 | tf_op jit(solution)/shard_map/all_to_all | solution.py:281
  32.8 0.5 total.1
  33.3 0.1 collective-permute-start
  33.4 1.3 %collective-permute-done.partner_ref = f32[256,128]{1,0:T(8,128)S(1)} collective-permute-done((f32[256,128]{1,0:T(8,128)S(1)}, f32[256,128]{1,0:T(8,128)S(1)}, u32[]{:S(2)}, u32[]{:S(2)}) %collective-permute-start) | collective-permute-done | bytes 131104 | tf_op jit(solution)/shard_map/ppermute | solution.py:290
  34.7 2.0 %collective-permute-start.1 = (f32[128,128]{1,0:T(8,128)S(1)}, f32[128,128]{1,0:T(8,128)S(1)}, u32[]{:S(2)}, u32[]{:S(2)}) collective-permute-start(f32[128,128]{1,0:T(8,128)S(1)} %get-tuple-element.10), channel_id=1, source_target_pairs={{0,32},{16,48},{32,64},{48,80},{64,96},{80,112},{96,0},{112,16},{1... | collective-permute-start | bytes 196616 | tf_op jit(solution)/shard_map/ppermute | solution.py:293
  36.7 3.6 %collective-permute-start.2 = (f32[128,128]{1,0:T(8,128)S(1)}, f32[128,128]{1,0:T(8,128)S(1)}, u32[]{:S(2)}, u32[]{:S(2)}) collective-permute-start(f32[128,128]{1,0:T(8,128)S(1)} %get-tuple-element.10), channel_id=1, source_target_pairs={{0,64},{16,80},{32,96},{48,112},{64,0},{80,16},{96,32},{112,48},{1... | collective-permute-start | bytes 196616 | tf_op jit(solution)/shard_map/ppermute | solution.py:293
  40.3 1.0 %collective-permute-start.3 = (f32[128,128]{1,0:T(8,128)S(1)}, f32[128,128]{1,0:T(8,128)S(1)}, u32[]{:S(2)}, u32[]{:S(2)}) collective-permute-start(f32[128,128]{1,0:T(8,128)S(1)} %get-tuple-element.10), channel_id=1, source_target_pairs={{0,96},{16,112},{32,0},{48,16},{64,32},{80,48},{96,64},{112,80},{1... | collective-permute-start | bytes 196616 | tf_op jit(solution)/shard_map/ppermute | solution.py:293
  41.3 0.0 copy-done
  41.3 0.7 local.1
  42.0 1.1 %collective-permute-start.4 = (f32[128,128]{1,0:T(8,128)S(1)}, f32[128,128]{1,0:T(8,128)S(1)}, u32[]{:S(2)}, u32[]{:S(2)}) collective-permute-start(f32[128,128]{1,0:T(8,128)S(1)} %get-tuple-element.9), channel_id=1, source_target_pairs={{0,32},{16,48},{32,64},{48,80},{64,96},{80,112},{96,0},{112,16},{1... | collective-permute-start | bytes 196616 | tf_op jit(solution)/shard_map/ppermute | solution.py:293
  43.1 0.5 collective-permute-start.5
  43.6 0.0 collective-permute-done.1.one_ref
  43.6 2.3 %collective-permute-start.6 = (f32[128,128]{1,0:T(8,128)S(1)}, f32[128,128]{1,0:T(8,128)S(1)}, u32[]{:S(2)}, u32[]{:S(2)}) collective-permute-start(f32[128,128]{1,0:T(8,128)S(1)} %get-tuple-element.9), channel_id=1, source_target_pairs={{0,96},{16,112},{32,0},{48,16},{64,32},{80,48},{96,64},{112,80},{1... | collective-permute-start | bytes 196616 | tf_op jit(solution)/shard_map/ppermute | solution.py:293
  45.9 0.0 collective-permute-done.2.two_ref
  45.9 0.0 collective-permute-done.3.three_ref
  45.9 12.2 %solve.1.solved_ref = f32[32,64,128]{2,1,0:T(8,128)S(1)} custom-call(s32[1]{0:T(128)} %bitcast.seq_ref, bf16[16,384,128]{2,1,0:T(8,128)(2,1)S(1)} %all_to_all.10.qkv_ref, f32[32,128,128]{2,1,0:T(8,128)S(1)} %get-tuple-element.7.gram_ref, f32[128,128]{1,0:T(8,128)S(1)} %collective-permute-done.1.one_ref, f32[128,128]{1,0:T(8,128)S(1)} %collective-permute-done.2.two_ref, ...), custom_call_target="tpu_custom_call" | custom-call | flops 10000000000 | bytes 31457280 | tf_op jit(solution)/shard_map/solve/pallas_call | solution.py:310
  58.1 0.0 collective-permute-done.4.one_ref
  58.1 0.0 collective-permute-done.5.two_ref
  58.1 0.0 collective-permute-done.6.three_ref
  58.1 1.5 %mix.1 = bf16[16,128,128]{2,1,0:T(8,128)(2,1)S(1)} custom-call(s32[1]{0:T(128)} %bitcast.seq_ref, f32[32,64,128]{2,1,0:T(8,128)S(1)} %solve.1.solved_ref, bf16[16,384,128]{2,1,0:T(8,128)(2,1)S(1)} %all_to_all.10.qkv_ref, f32[32,128,128]{2,1,0:T(8,128)S(1)} %get-tuple-element.8.vk_ref, f32[128,128]{1,0:T(8,128)S(1)} %collective-permute-done.4.one_ref, ...), custom_call_target="tpu_custom_call" | custom-call | tf_op jit(solution)/shard_map/mix/pallas_call | solution.py:326
  59.7 13.4 %all_to_all.11.mixed_hbm = bf16[16,128,128]{2,1,0:T(8,128)(2,1)S(1)} all-to-all(bf16[16,128,128]{2,1,0:T(8,128)(2,1)S(1)} %mix.1), channel_id=1, replica_groups=mesh['seq'=8,'head'=16] {'head'}, dimensions={0} | all-to-all | bytes 1048576 | tf_op jit(solution)/shard_map/all_to_all | solution.py:335
  73.1 0.9 %to_tokens.1 = bf16[128,2048]{1,0:T(8,128)(2,1)} custom-call(bf16[16,128,128]{2,1,0:T(8,128)(2,1)S(1)} %all_to_all.11.mixed_hbm), custom_call_target="tpu_custom_call" | custom-call | tf_op jit(solution)/shard_map/to_tokens/pallas_call | solution.py:336
  (2 shorter events, 0.0 us)
Async XLA Ops:
  0.0 41.3 %copy-start = (f32[16,128]{1,0:T(8,128)S(1)}, f32[16,128]{1,0:T(8,128)}, u32[]{:S(2)}) copy-start(f32[16,128]{1,0:T(8,128)} %param.7) | copy-start | bytes 24580
  33.3 1.4 %collective-permute-start = (f32[256,128]{1,0:T(8,128)S(1)}, f32[256,128]{1,0:T(8,128)S(1)}, u32[]{:S(2)}, u32[]{:S(2)}) collective-permute-start(f32[256,128]{1,0:T(8,128)S(1)} %total.1), channel_id=1, source_target_pairs={{0,16},{16,0},{32,48},{48,32},{64,80},{80,64},{96,112},{112,96},{1... | collective-permute-start | bytes 393224 | tf_op jit(solution)/shard_map/ppermute | solution.py:290
  34.7 8.9 %collective-permute-start.1 = (f32[128,128]{1,0:T(8,128)S(1)}, f32[128,128]{1,0:T(8,128)S(1)}, u32[]{:S(2)}, u32[]{:S(2)}) collective-permute-start(f32[128,128]{1,0:T(8,128)S(1)} %get-tuple-element.10), channel_id=1, source_target_pairs={{0,32},{16,48},{32,64},{48,80},{64,96},{80,112},{96,0},{112,16},{1... | collective-permute-start | bytes 196616 | tf_op jit(solution)/shard_map/ppermute | solution.py:293
  36.7 9.2 %collective-permute-start.2 = (f32[128,128]{1,0:T(8,128)S(1)}, f32[128,128]{1,0:T(8,128)S(1)}, u32[]{:S(2)}, u32[]{:S(2)}) collective-permute-start(f32[128,128]{1,0:T(8,128)S(1)} %get-tuple-element.10), channel_id=1, source_target_pairs={{0,64},{16,80},{32,96},{48,112},{64,0},{80,16},{96,32},{112,48},{1... | collective-permute-start | bytes 196616 | tf_op jit(solution)/shard_map/ppermute | solution.py:293
  40.3 5.6 %collective-permute-start.3 = (f32[128,128]{1,0:T(8,128)S(1)}, f32[128,128]{1,0:T(8,128)S(1)}, u32[]{:S(2)}, u32[]{:S(2)}) collective-permute-start(f32[128,128]{1,0:T(8,128)S(1)} %get-tuple-element.10), channel_id=1, source_target_pairs={{0,96},{16,112},{32,0},{48,16},{64,32},{80,48},{96,64},{112,80},{1... | collective-permute-start | bytes 196616 | tf_op jit(solution)/shard_map/ppermute | solution.py:293
  42.0 16.1 %collective-permute-start.4 = (f32[128,128]{1,0:T(8,128)S(1)}, f32[128,128]{1,0:T(8,128)S(1)}, u32[]{:S(2)}, u32[]{:S(2)}) collective-permute-start(f32[128,128]{1,0:T(8,128)S(1)} %get-tuple-element.9), channel_id=1, source_target_pairs={{0,32},{16,48},{32,64},{48,80},{64,96},{80,112},{96,0},{112,16},{1... | collective-permute-start | bytes 196616 | tf_op jit(solution)/shard_map/ppermute | solution.py:293
  43.1 15.0 %collective-permute-start.5 = (f32[128,128]{1,0:T(8,128)S(1)}, f32[128,128]{1,0:T(8,128)S(1)}, u32[]{:S(2)}, u32[]{:S(2)}) collective-permute-start(f32[128,128]{1,0:T(8,128)S(1)} %get-tuple-element.9), channel_id=1, source_target_pairs={{0,64},{16,80},{32,96},{48,112},{64,0},{80,16},{96,32},{112,48},{1... | collective-permute-start | bytes 196616 | tf_op jit(solution)/shard_map/ppermute | solution.py:293
  43.6 14.5 %collective-permute-start.6 = (f32[128,128]{1,0:T(8,128)S(1)}, f32[128,128]{1,0:T(8,128)S(1)}, u32[]{:S(2)}, u32[]{:S(2)}) collective-permute-start(f32[128,128]{1,0:T(8,128)S(1)} %get-tuple-element.9), channel_id=1, source_target_pairs={{0,96},{16,112},{32,0},{48,16},{64,32},{80,48},{96,64},{112,80},{1... | collective-permute-start | bytes 196616 | tf_op jit(solution)/shard_map/ppermute | solution.py:293
